TPU v7x, 128 devices: a whole 4x4x4 slice. The times are simulated.
128 devices in a mesh: shot: 8 (over z, core), rline: 16 (over y, x).
Axes of the slice: x: 4, y: 4, z: 4, core: 2. Of those that a mesh axis runs over, the one named last changes fastest.
Arguments:
- traces: bfloat16 [32, 1536, 1024], P('shot', 'rline'), may hold values from -6 to 6
- kernels_shot: bfloat16 [4, 15, 31], replicated, may hold values from -0.25 to 0.25
- kernels_rcv: bfloat16 [4, 15, 31], replicated, may hold values from -0.25 to 0.25
- dest: int32 [32, 1536], P('shot', 'rline'), may hold values from -1 to 127, as said below
- gather: int32 [32, 1536], P('shot', 'rline'), may hold values from -1 to 11, as said below
- fold: int32 [32, 1536], P('shot', 'rline'), may hold values from -1 to 31, as said below
- counts: int32 [1536], P(('shot', 'rline')), may hold values from 1 to 32, as said below
Outputs:
- filtered: float32 [32, 1536, 1024], P('shot', 'rline')
Inputs may be any that keep to these rules, and one draw needn't show every extreme that they name: `dest`: A live trace names the index, on the shot and rline axes taken together (shot index times the rline size plus rline index), of the device that owns its receiver's gather. All live traces of one receiver name the same owner; every device owns exactly 12 receivers, at most 1 of them among the receivers of one rline index; every receiver has a live trace. `gather`: the 12 receivers of one owner carry distinct numbers; -1 exactly where dest is -1. `fold`: the number of live traces of the same receiver with a lower shot index; -1 exactly where dest is -1. Every owner has one receiver all of whose traces are live. `counts`: entry o * 12 + k is the number of live traces of the receiver with owner o and gather number k.
All inputs are finite; a program needn't handle non-finite values.
Results may differ from a plain program's by a relative error of at most 0.0032.
Values may be sent and summed in bfloat16 or wider, within the bound.
A program may use at most 64 MiB of HBM per device.

v0:
```python
import jax
import jax.numpy as jnp
from jax import lax
from jax.sharding import PartitionSpec as P

WINDOW = 256
BLOCK_WIDTH = 128


def padded_2(cells, sides, width):
    for axis, dim in sides:
        count = lax.axis_size(axis)
        ends = count - 1
        head = lax.slice_in_dim(cells, 0, width, axis=dim)
        tail = lax.slice_in_dim(cells, cells.shape[dim] - width, cells.shape[dim], axis=dim)
        cells = jnp.concatenate(
            [
                lax.ppermute(tail, axis, [(i, (i + 1) % count) for i in range(ends)]),
                cells,
                lax.ppermute(head, axis, [((i + 1) % count, i) for i in range(ends)]),
            ],
            axis=dim,
        )
    return cells


def banded_table(kernels):
    fan_count, trace_reach, tap_count = kernels.shape
    shape = (WINDOW, BLOCK_WIDTH, tap_count)
    row_index = lax.broadcasted_iota(jnp.int32, shape, 0)
    col_index = lax.broadcasted_iota(jnp.int32, shape, 1)
    lag_index = lax.broadcasted_iota(jnp.int32, shape, 2)
    offset = (WINDOW - BLOCK_WIDTH) // 2 - (tap_count - 1) // 2
    picker = (row_index - col_index - offset == lag_index).astype(jnp.float32)
    banded = jnp.einsum(
        "uts,fas->auft", picker, kernels.astype(jnp.float32), precision=lax.Precision.HIGHEST
    )
    return banded.reshape(trace_reach, WINDOW, fan_count * BLOCK_WIDTH).astype(jnp.bfloat16)


def dip_subtract(padded, banded, trace_reach):
    groups, padded_rows, samples = padded.shape
    length = padded_rows - (trace_reach - 1)
    rim_width = (trace_reach - 1) // 2
    blocks = samples // BLOCK_WIDTH
    sample_margin = (WINDOW - BLOCK_WIDTH) // 2
    fan_count = banded.shape[2] // BLOCK_WIDTH
    widened = jnp.pad(padded, ((0, 0), (0, 0), (sample_margin, sample_margin)))

    def one_block(index, result):
        start = index * BLOCK_WIDTH
        window = lax.dynamic_slice_in_dim(widened, start, WINDOW, 2)
        coherent = jnp.zeros((groups, length, fan_count * BLOCK_WIDTH), jnp.float32)
        for shift in range(trace_reach):
            coherent = coherent + jnp.einsum(
                "roh,hn->ron",
                window[:, shift : shift + length],
                banded[shift],
                preferred_element_type=jnp.float32,
            )
        coherent = coherent.reshape(groups, length, fan_count, BLOCK_WIDTH)
        energy = jnp.sum(coherent * coherent, axis=2)
        centre = window[
            :, rim_width : rim_width + length, sample_margin : sample_margin + BLOCK_WIDTH
        ].astype(jnp.float32)
        value = centre - jnp.sum(coherent * coherent * coherent, axis=2) / (energy + 1.0)
        return lax.dynamic_update_slice_in_dim(result, value, start, 2)

    initial = jnp.zeros((groups, length, samples), jnp.float32)
    return lax.fori_loop(0, blocks, one_block, initial)


def shards(traces, kernels_shot, kernels_rcv, dest, gather, fold, counts):
    shot_dev, rcv_dev, samples = traces.shape
    shot_size = lax.axis_size("shot")
    rline_size = lax.axis_size("rline")
    devices = shot_size * rline_size
    trace_reach = kernels_shot.shape[1]
    rim_width = (trace_reach - 1) // 2
    fold_cap = shot_dev * shot_size
    gathers_dev = rcv_dev // shot_size
    per_block = (rcv_dev + devices - 1) // devices
    capacity = shot_dev * per_block
    alive_mask = dest >= 0
    cleaned = jnp.where(alive_mask[..., None], traces, jnp.zeros_like(traces))
    padded = padded_2(cleaned, (("rline", 1),), rim_width)
    first_pass = dip_subtract(padded, banded_table(kernels_shot), trace_reach).astype(jnp.bfloat16)
    self_index = lax.broadcasted_iota(jnp.int32, (rcv_dev, rcv_dev), 0)
    peer_index = lax.broadcasted_iota(jnp.int32, (rcv_dev, rcv_dev), 1)
    same_owner = (dest[:, :, None] == dest[:, None, :]) & (peer_index < self_index)[None]
    slot_rank = jnp.sum(same_owner.astype(jnp.int32), axis=2)
    shot_row = lax.broadcasted_iota(jnp.int32, dest.shape, 0)
    send_slot = dest * capacity + shot_row * per_block + slot_rank
    flat_slot = jnp.where(alive_mask, send_slot, devices * capacity).reshape(-1)
    outgoing = (
        jnp.zeros((devices * capacity, samples), jnp.bfloat16)
        .at[flat_slot]
        .set(first_pass.reshape(-1, samples), mode="drop")
    )
    labels_out = (
        jnp.full((devices * capacity,), -1, jnp.int32)
        .at[flat_slot]
        .set((gather * fold_cap + fold).reshape(-1), mode="drop")
    )
    arrived, labels = (
        lax.all_to_all(
            outgoing.reshape(devices, capacity, samples),
            ("shot", "rline"),
            split_axis=0,
            concat_axis=0,
            tiled=True,
        ),
        lax.all_to_all(
            labels_out.reshape(devices, capacity),
            ("shot", "rline"),
            split_axis=0,
            concat_axis=0,
            tiled=True,
        ),
    )
    labels = labels.reshape(-1)
    arrived = arrived.reshape(-1, samples)
    target = jnp.where(labels >= 0, labels, gathers_dev * fold_cap)
    receiver_stacks = (
        jnp.zeros((gathers_dev * fold_cap, samples), jnp.bfloat16)
        .at[target]
        .set(arrived, mode="drop")
    )
    receiver_stacks = receiver_stacks.reshape(gathers_dev, fold_cap, samples)
    stack_padded = jnp.pad(receiver_stacks, ((0, 0), (rim_width, rim_width), (0, 0)))
    second_pass = dip_subtract(stack_padded, banded_table(kernels_rcv), trace_reach)
    fold_gain = jnp.sqrt(fold_cap / counts.astype(jnp.float32))
    second_pass = (second_pass * fold_gain[:, None, None]).reshape(-1, samples)
    returning = jnp.where((labels >= 0)[:, None], second_pass[jnp.maximum(labels, 0)], 0.0)
    returned = lax.all_to_all(
        returning.reshape(devices, capacity, samples),
        ("shot", "rline"),
        split_axis=0,
        concat_axis=0,
        tiled=True,
    )
    returned = returned.reshape(-1, samples)
    picked = returned[jnp.minimum(flat_slot, devices * capacity - 1)]
    result = jnp.where(alive_mask.reshape(-1)[:, None], picked, 0.0)
    return result.reshape(shot_dev, rcv_dev, samples)


def solution(mesh):
    in_specs = (
        P("shot", "rline", None),
        P(),
        P(),
        P("shot", "rline"),
        P("shot", "rline"),
        P("shot", "rline"),
        P(("shot", "rline")),
    )
    out_specs = P("shot", "rline", None)
    return jax.shard_map(shards, mesh=mesh, in_specs=in_specs, out_specs=out_specs, check_vma=False)
```

profile of v0, /device:TPU:1, one launch (start us, length us, event | category | flops | bytes accessed | tf_op | source)
XLA Modules:
  0.0 512.9 jit_solution(16483893751224586676)
XLA Ops:
  2.0 3.9 collective-permute-start
  9.8 2.9 scatter_custom_fusion
  13.5 12.1 %all-to-all-start = ((s32[128,1,4]{2,1,0:T(1,128)}), s32[128,1,4]{2,1,0:T(1,128)S(1)}, u32[]{:S(2)}, u32[]{:S(2)}) async-start(s32[128,1,4]{2,1,0:T(1,128)} %bitcast.60), calls=%async_computation | async-start | bytes 131072 | tf_op jit(solution)/shard_map/all_to_all | solution.py:113
  25.6 3.9 convert_bitcast_fusion.1
  29.5 7.9 %copy.45 = bf16[15,256,4,128]{1,3,2,0:T(8,128)(2,1)} copy(bf16[15,256,4,128]{3,0,2,1:T(8,128)(2,1)} %convert_bitcast_fusion.1) | data formatting | bytes 7864320 | tf_op jit(solution)/shard_map/convert_element_type | solution.py:38
  37.3 6.3 %copy.46 = bf16[15,256,512]{2,1,0:T(8,128)(2,1)} copy(bf16[15,256,512]{1,2,0:T(8,128)(2,1)} %bitcast.212) | data formatting | bytes 7864320 | tf_op jit(solution)/shard_map/while | solution.py:70
  45.3 186.8 %while.26 = (s32[]{:T(128)}, bf16[4,96,1024]{2,1,0:T(8,128)(2,1)}, bf16[4,110,1152]{2,1,0:T(8,128)(2,1)S(1)}, bf16[15,256,512]{2,1,0:T(8,128)(2,1)}, s32[]{:T(12...) while((s32[]{:T(128)}, bf16[4,96,1024]{2,1,0:T(8,128)(2,1)}, ...), condition=%wide.region_5.6_spmd, body=%wide.region_2.5_spmd.sunk | while | flops 1513586688 | bytes 33129040 | solution.py:70
  54.2 2.2 convolution_add_fusion.62
  61.7 2.2 convolution_add_fusion.67
  77.6 2.2 convolution_add_fusion.62
  85.0 2.2 convolution_add_fusion.67
  87.2 1.5 convolution_add_fusion.68
  100.9 2.2 convolution_add_fusion.62
  108.4 2.2 convolution_add_fusion.67
  110.5 1.5 convolution_add_fusion.68
  124.3 2.2 convolution_add_fusion.62
  131.8 2.2 convolution_add_fusion.67
  147.6 2.2 convolution_add_fusion.62
  155.1 2.2 convolution_add_fusion.67
  171.0 2.2 convolution_add_fusion.62
  178.4 2.2 convolution_add_fusion.67
  180.6 1.5 convolution_add_fusion.68
  194.3 2.2 convolution_add_fusion.62
  201.8 2.2 convolution_add_fusion.67
  204.0 1.5 convolution_add_fusion.68
  217.7 2.2 convolution_add_fusion.62
  225.2 2.2 convolution_add_fusion.67
  232.2 3.1 scatter_custom_fusion.1
  236.5 9.8 %all-to-all-start.1 = ((bf16[128,4,1024]{2,1,0:T(4,128)(2,1)}), bf16[128,4,1024]{2,1,0:T(4,128)(2,1)S(1)}, u32[]{:S(2)}, u32[]{:S(2)}) async-start(bf16[128,4,1024]{2,1,0:T(4,128)(2,1)} %reshape.172), calls=%async_computation.1 | async-start | bytes 2097152 | tf_op jit(solution)/shard_map/all_to_all | solution.py:106
  246.3 3.2 convert_bitcast_fusion
  249.5 7.9 %copy.48 = bf16[15,256,4,128]{1,3,2,0:T(8,128)(2,1)} copy(bf16[15,256,4,128]{3,0,2,1:T(8,128)(2,1)} %convert_bitcast_fusion) | data formatting | bytes 7864320 | tf_op jit(solution)/shard_map/convert_element_type | solution.py:38
  257.4 6.3 %copy.49 = bf16[15,256,512]{2,1,0:T(8,128)(2,1)} copy(bf16[15,256,512]{1,2,0:T(8,128)(2,1)} %bitcast.213) | data formatting | bytes 7864320 | tf_op jit(solution)/shard_map/while | solution.py:70
  265.7 2.9 scatter_custom_fusion.2
  270.7 187.3 %while.27 = (s32[]{:T(128)}, f32[12,32,1024]{2,1,0:T(8,128)}, bf16[12,46,1152]{2,1,0:T(8,128)(2,1)S(1)}, bf16[15,256,512]{2,1,0:T(8,128)(2,1)}, s32[]{:T(128)}, ...) while((s32[]{:T(128)}, f32[12,32,1024]{2,1,0:T(8,128)}, ...), condition=%wide.region_11.12_spmd, body=%wide.region_8.11_spmd.sunk | while | flops 1513586688 | bytes 33129040 | solution.py:70
  279.6 2.2 convolution_add_fusion.76
  287.1 2.2 convolution_add_fusion.81
  289.2 1.5 convolution_add_fusion.82
  303.0 2.2 convolution_add_fusion.76
  310.5 2.2 convolution_add_fusion.81
  312.6 1.5 convolution_add_fusion.82
  326.4 2.2 convolution_add_fusion.76
  333.9 2.2 convolution_add_fusion.81
  336.1 1.5 convolution_add_fusion.82
  349.9 2.2 convolution_add_fusion.76
  357.3 2.2 convolution_add_fusion.81
  373.3 2.2 convolution_add_fusion.76
  380.7 2.2 convolution_add_fusion.81
  396.7 2.2 convolution_add_fusion.76
  404.2 2.2 convolution_add_fusion.81
  406.3 1.5 convolution_add_fusion.82
  420.1 2.2 convolution_add_fusion.76
  427.6 2.2 convolution_add_fusion.81
  429.8 1.5 convolution_add_fusion.82
  443.6 2.2 convolution_add_fusion.76
  451.0 2.2 convolution_add_fusion.81
  458.1 1.6 broadcast_multiply_fusion
  459.7 2.7 gather_fusion
  462.4 1.9 gather.11
  464.3 1.8 broadcast_select_fusion
  466.1 10.2 %all-to-all-start.2 = ((f32[128,4,1024]{2,1,0:T(4,128)}), f32[128,4,1024]{2,1,0:T(4,128)}, u32[]{:S(2)}, u32[]{:S(2)}) async-start(f32[128,4,1024]{2,1,0:T(4,128)} %broadcast_select_fusion), calls=%async_computation.2 | async-start | bytes 4194304 | tf_op jit(solution)/shard_map/all_to_all | solution.py:135
  476.4 29.3 %all-to-all-done.2 = f32[128,4,1024]{2,1,0:T(4,128)} async-done(((f32[128,4,1024]{2,1,0:T(4,128)}), f32[128,4,1024]{2,1,0:T(4,128)}, u32[]{:S(2)}, u32[]{:S(2)}) %all-to-all-start.2) | async-done | bytes 2097184 | tf_op jit(solution)/shard_map/all_to_all | solution.py:135
  505.7 2.0 reshape.176
  507.7 2.5 gather_fusion.1
  510.2 2.7 broadcast_select_fusion.1
  (283 shorter events, 303.2 us)
Async XLA Ops:
  2.0 41.7 %collective-permute-start = (bf16[4,7,1024]{2,1,0:T(8,128)(2,1)S(1)}, bf16[4,7,1024]{2,1,0:T(8,128)(2,1)S(1)}, u32[]{:S(2)}, u32[]{:S(2)}) collective-permute-start(bf16[4,7,1024]{2,1,0:T(8,128)(2,1)S(1)} %get-tuple-element.227), channel_id=1, source_target_pairs={{0,1},{1,2},{2,3},{3,4},{4,5},{5,6},{6,7},{7,8},{8,9},{9,10},{10,1... | collective-permute-start | bytes 172040 | tf_op jit(solution)/shard_map/ppermute | solution.py:18
  5.9 37.7 %collective-permute-start.1 = (bf16[4,7,1024]{2,1,0:T(8,128)(2,1)S(1)}, bf16[4,7,1024]{2,1,0:T(8,128)(2,1)S(1)}, u32[]{:S(2)}, u32[]{:S(2)}) collective-permute-start(bf16[4,7,1024]{2,1,0:T(8,128)(2,1)S(1)} %get-tuple-element.228), channel_id=1, source_target_pairs={{1,0},{2,1},{3,2},{4,3},{5,4},{6,5},{7,6},{8,7},{9,8},{10,9},{11,1... | collective-permute-start | bytes 172040 | tf_op jit(solution)/shard_map/ppermute | solution.py:20
  13.5 223.0 %all-to-all-start = ((s32[128,1,4]{2,1,0:T(1,128)}), s32[128,1,4]{2,1,0:T(1,128)S(1)}, u32[]{:S(2)}, u32[]{:S(2)}) async-start(s32[128,1,4]{2,1,0:T(1,128)} %bitcast.60), calls=%async_computation | async-start | bytes 131072 | tf_op jit(solution)/shard_map/all_to_all | solution.py:113
  232.2 14.1 %copy-start = (bf16[4,15,31]{2,0,1:T(4,128)(2,1)S(1)}, bf16[4,15,31]{2,0,1:T(4,128)(2,1)}, u32[]{:S(2)}) copy-start(bf16[4,15,31]{2,0,1:T(4,128)(2,1)} %param.13) | copy-start | bytes 11164
  236.5 28.9 %all-to-all-start.1 = ((bf16[128,4,1024]{2,1,0:T(4,128)(2,1)}), bf16[128,4,1024]{2,1,0:T(4,128)(2,1)S(1)}, u32[]{:S(2)}, u32[]{:S(2)}) async-start(bf16[128,4,1024]{2,1,0:T(4,128)(2,1)} %reshape.172), calls=%async_computation.1 | async-start | bytes 2097152 | tf_op jit(solution)/shard_map/all_to_all | solution.py:106
  257.4 6.3 %copy-start.1 = (s32[12]{0:T(128)S(1)}, s32[12]{0:T(128)}, u32[]{:S(2)}) copy-start(s32[12]{0:T(128)} %param.17) | copy-start | bytes 148
  466.1 39.6 %all-to-all-start.2 = ((f32[128,4,1024]{2,1,0:T(4,128)}), f32[128,4,1024]{2,1,0:T(4,128)}, u32[]{:S(2)}, u32[]{:S(2)}) async-start(f32[128,4,1024]{2,1,0:T(4,128)} %broadcast_select_fusion), calls=%async_computation.2 | async-start | bytes 4194304 | tf_op jit(solution)/shard_map/all_to_all | solution.py:135
where the time goes:
time: 521 us; the launch traced here: 513 us
  matrix products  347 us (67%)
  local copies, waits for them, and re-layouts  57 us (11%)
  other arithmetic  40.5 us (8%)
  starting transfers between devices  37.3 us (7%)
  waiting for transfers between devices  29.4 us (6%)
    dot_general x240, matrix products, one_block(): jnp.einsum('roh,hn->ron', window[:, shift:shift + length], banded[shift],...  340 us
    all_to_all x1, waiting for transfers between devices, shards(): lax.all_to_all(returning.reshape(devices, capacity, samples), ('shot', 'r...  29.3 us
    convert_element_type x2, local copies, waits for them, and re-layouts, banded_table(): banded.reshape(trace_reach, WINDOW, fan_count * BLOCK_WIDTH)  15.7 us
    reduce_sum x16, other arithmetic, one_block(): energy = jnp.sum(coherent * coherent, axis=2)  15.6 us
    dynamic_update_slice x16, other arithmetic, one_block(): return lax.dynamic_update_slice_in_dim(result, value, start, 2)  12.8 us
    while x2, local copies, waits for them, and re-layouts, dip_subtract(): return lax.fori_loop(0, blocks, one_block, initial)  12.6 us
    all_to_all x1, starting transfers between devices, shards(): lax.all_to_all(labels_out.reshape(devices, capacity), ('shot', 'rline'),...  12.1 us
  transfers between devices with their start and end apart: 5, of which 1 were waited for; matrix products, arithmetic and copies ran while one was open for 46% of the time, Pallas kernels for 0%

commit v1 on v0

v1 whole, which is shorter than its diff:
```python
import functools

import jax
import jax.numpy as jnp
from jax import lax
from jax.experimental import pallas as pl
from jax.experimental.pallas import tpu as pltpu
from jax.sharding import PartitionSpec as P

LANES = 128
CHUNKS = 8
BF16 = jnp.bfloat16
F32 = jnp.float32


def lane_index(shape):
    return lax.broadcasted_iota(jnp.int32, shape, len(shape) - 1)


def build_table(kernel_ref, table_ref):
    taps = kernel_ref.shape[2]
    tap = lax.broadcasted_iota(jnp.int32, (taps, LANES), 0)
    lane = lax.broadcasted_iota(jnp.int32, (taps, LANES), 1)
    place_low = (lane == LANES - 1 - tap).astype(BF16)
    place_high = (lane == LANES // 2 - 1 - tap).astype(BF16)
    even = (lane_index((64, LANES)) // 32) % 2 == 0
    for half in range(2):
        base = jnp.dot(kernel_ref[2 * half], place_low, preferred_element_type=F32) + jnp.dot(
            kernel_ref[2 * half + 1], place_high, preferred_element_type=F32
        )
        before = jnp.zeros((64, LANES), F32)
        for step in range(16):
            if step < 15:
                row = jnp.broadcast_to(base[step : step + 1], (64, LANES))
                here = pltpu.roll(row, 0, 1, stride=1, stride_axis=0)
            else:
                here = jnp.zeros((64, LANES), F32)
            block = jnp.where(even, here, pltpu.roll(before, 32, 1))
            table_ref[step * 64 : (step + 1) * 64, half * LANES : (half + 1) * LANES] = block.astype(BF16)
            before = here


def windows(first, second):
    shape = first.shape
    lane = lane_index(shape)
    chunk = lax.broadcasted_iota(jnp.int32, shape, 1)
    low = lane < 64

    def both(x):
        left = jnp.where(chunk == 0, 0.0, pltpu.roll(x, 1, 1))
        right = jnp.where(chunk == CHUNKS - 1, 0.0, pltpu.roll(x, CHUNKS - 1, 1))
        early = pltpu.roll(jnp.where(lane < 112, x, left), 16, 2)
        late = pltpu.roll(jnp.where(lane >= 16, x, right), 112, 2)
        return early, late

    early_a, late_a = both(first)
    early_b, late_b = both(second)
    return (
        jnp.where(low, early_a, pltpu.roll(early_b, 64, 2)),
        jnp.where(low, late_a, pltpu.roll(late_b, 64, 2)),
        jnp.where(low, pltpu.roll(early_a, 64, 2), early_b),
        jnp.where(low, pltpu.roll(late_a, 64, 2), late_b),
    )


def fan_terms(window_ref, table_ref, start, pairs):
    rows = pairs * 16
    left = jnp.concatenate(
        [
            jnp.concatenate(
                [window_ref[quarter, pl.ds(start + step, pairs)].reshape(rows, LANES) for step in range(8)],
                axis=1,
            )
            for quarter in range(4)
        ],
        axis=0,
    )
    coherent = jnp.dot(left, table_ref[...], preferred_element_type=F32)
    squares, cubes = [], []
    for quarter in range(4):
        part = coherent[quarter * rows : (quarter + 1) * rows]
        one, two = part[:, :LANES], part[:, LANES:]
        one_sq, two_sq = one * one, two * two
        squares.append(one_sq + two_sq)
        cubes.append(one_sq * one + two_sq * two)
    lane = lane_index((rows, LANES))
    low = lane < 64
    even = (lane // 32) % 2 == 0

    def merged(s):
        s02, s20 = jnp.where(low, s[0], s[2]), jnp.where(low, s[2], s[0])
        s13, s31 = jnp.where(low, s[1], s[3]), jnp.where(low, s[3], s[1])
        a = jnp.where(even, s02, s13) + pltpu.roll(jnp.where(even, s20, s31), 64, 1)
        b = jnp.where(even, s13, s02) + pltpu.roll(jnp.where(even, s31, s20), 64, 1)
        return a, b

    square_a, square_b = merged(squares)
    cube_a, cube_b = merged(cubes)
    term_a = cube_a / (square_a + 1.0)
    term_b = cube_b / (square_b + 1.0)
    return (
        jnp.where(even, term_a, pltpu.roll(term_b, 32, 1)),
        jnp.where(even, pltpu.roll(term_b, 96, 1), term_a),
    )


def shot_kernel(x_ref, kernel_ref, out_ref, window_ref, table_ref):
    build_table(kernel_ref, table_ref)
    groups, padded = x_ref.shape[0], x_ref.shape[1]
    step_pairs = 5
    pairs = 8

    @pl.loop(0, groups)
    def _(g):
        @pl.loop(0, padded // (2 * step_pairs))
        def _(i):
            x = x_ref[g, pl.ds(i * 2 * step_pairs, 2 * step_pairs)].astype(F32)
            x = x.reshape(step_pairs, 2, 2, CHUNKS, LANES)
            first = x[:, 0].reshape(step_pairs * 2, CHUNKS, LANES)
            second = x[:, 1].reshape(step_pairs * 2, CHUNKS, LANES)
            for quarter, tile in enumerate(windows(first, second)):
                window_ref[quarter, pl.ds(i * step_pairs, step_pairs)] = tile.reshape(
                    step_pairs, 16, LANES
                ).astype(BF16)

        @pl.loop(0, out_ref.shape[1] // (2 * pairs))
        def _(i):
            start = i * pairs
            even, odd = fan_terms(window_ref, table_ref, start, pairs)
            terms = jnp.stack(
                [even.reshape(pairs, 16, LANES), odd.reshape(pairs, 16, LANES)], axis=1
            ).reshape(2 * pairs, 16, LANES)
            centre = x_ref[g, pl.ds(2 * start + 7, 2 * pairs)].astype(F32)
            out_ref[g, pl.ds(2 * start, 2 * pairs)] = (centre - terms).astype(BF16)


def receiver_kernel(x_ref, fold_ref, kernel_ref, out_ref, window_ref, table_ref, stack_ref, pick_ref):
    build_table(kernel_ref, table_ref)
    sources, groups, receivers = x_ref.shape[0], x_ref.shape[1], x_ref.shape[2]
    shots = sources * groups * 2
    rows = shots * CHUNKS
    pairs = shots // 2
    stack_ref[0:7] = jnp.zeros((7, 16, LANES), F32)
    stack_ref[7 + shots : 16 + shots] = jnp.zeros((9, 16, LANES), F32)
    place = lax.broadcasted_iota(jnp.int32, (rows, rows), 0)

    @pl.loop(0, receivers // 2)
    def _(g):
        gains = []
        for side in range(2):
            k = 2 * g + side
            labels = fold_ref[k]
            pick = (labels == place).astype(F32).astype(BF16)
            pick_ref[side] = pick
            live = jnp.sum((labels >= 0).astype(F32), axis=1, keepdims=True) / CHUNKS
            gains.append(jnp.sqrt(shots / live))
            x = x_ref[:, :, k].reshape(rows, LANES)
            stack = jnp.dot(pick, x, preferred_element_type=F32).reshape(shots, CHUNKS, LANES)
            stack_ref[7 : 7 + shots, side * CHUNKS : (side + 1) * CHUNKS] = stack
        step_pairs = 6

        @pl.loop(0, 4)
        def _(i):
            x = stack_ref[pl.ds(i * 2 * step_pairs, 2 * step_pairs)]
            x = x.reshape(step_pairs, 2, 2, CHUNKS, LANES)
            first = x[:, 0].reshape(step_pairs * 2, CHUNKS, LANES)
            second = x[:, 1].reshape(step_pairs * 2, CHUNKS, LANES)
            for quarter, tile in enumerate(windows(first, second)):
                window_ref[quarter, pl.ds(i * step_pairs, step_pairs)] = tile.reshape(
                    step_pairs, 16, LANES
                ).astype(BF16)

        value = []
        for half in range(2):
            count = pairs // 2
            start = half * count
            even, odd = fan_terms(window_ref, table_ref, start, count)
            terms = jnp.stack(
                [even.reshape(count, 16, LANES), odd.reshape(count, 16, LANES)], axis=1
            ).reshape(2 * count, 16, LANES)
            value.append(stack_ref[7 + 2 * start : 7 + 2 * start + 2 * count] - terms)
        value = jnp.concatenate(value, axis=0)
        for side in range(2):
            k = 2 * g + side
            own = value[:, side * CHUNKS : (side + 1) * CHUNKS].reshape(rows, LANES) * gains[side]
            back = lax.dot_general(
                pick_ref[side], own.astype(BF16), (((0,), (0,)), ((), ())), preferred_element_type=F32
            )
            out_ref[:, :, k] = back.astype(BF16).reshape(sources, groups, 16, LANES)


def vmem():
    return pl.BlockSpec(memory_space=pltpu.VMEM)


def shards(traces, kernels_shot, kernels_rcv, dest, gather, fold, counts):
    shot_dev, rcv_dev, samples = traces.shape
    shot_size = lax.axis_size("shot")
    rline_size = lax.axis_size("rline")
    shots = shot_dev * shot_size
    own = rcv_dev // shot_size
    rim = 7
    limit = 48 << 20

    fold_all = lax.all_gather(fold, "shot", axis=0, tiled=True)
    cleaned = jnp.where((dest >= 0)[..., None], traces, jnp.zeros_like(traces))
    head, tail = cleaned[:, :rim], cleaned[:, rcv_dev - rim :]
    ends = rline_size - 1
    padded = jnp.concatenate(
        [
            lax.ppermute(tail, "rline", [(i, i + 1) for i in range(ends)]),
            cleaned,
            lax.ppermute(head, "rline", [(i + 1, i) for i in range(ends)]),
        ],
        axis=1,
    )
    groups = shot_dev // 2
    x = padded.reshape(groups, 2, rcv_dev + 2 * rim, CHUNKS, LANES).transpose(0, 2, 1, 3, 4)
    x = x.reshape(groups, rcv_dev + 2 * rim, 16, LANES)
    pair_count = (rcv_dev + 2 * rim) // 2
    first_pass = pl.pallas_call(
        shot_kernel,
        out_shape=jax.ShapeDtypeStruct((groups, rcv_dev, 16, LANES), BF16),
        in_specs=[vmem(), vmem()],
        out_specs=vmem(),
        scratch_shapes=[
            pltpu.VMEM((4, pair_count, 16, LANES), BF16),
            pltpu.VMEM((1024, 256), BF16),
        ],
        compiler_params=pltpu.CompilerParams(vmem_limit_bytes=limit),
    )(x, kernels_shot)

    mine = lax.dynamic_slice_in_dim(fold_all, lax.axis_index("shot") * own, own, 1)
    spread = jnp.where(mine >= 0, mine * CHUNKS, -64).T[:, :, None] + jnp.arange(CHUNKS, dtype=jnp.int32)
    labels = spread.reshape(own, 1, shots * CHUNKS)

    sent = first_pass.reshape(groups, shot_size, own, 16, LANES)
    arrived = lax.all_to_all(sent, "shot", split_axis=1, concat_axis=0, tiled=False)
    back = pl.pallas_call(
        receiver_kernel,
        out_shape=jax.ShapeDtypeStruct((shot_size, groups, own, 16, LANES), BF16),
        in_specs=[vmem(), vmem(), vmem()],
        out_specs=vmem(),
        scratch_shapes=[
            pltpu.VMEM((4, shots // 2 + 8, 16, LANES), BF16),
            pltpu.VMEM((1024, 256), BF16),
            pltpu.VMEM((shots + 16, 16, LANES), F32),
            pltpu.VMEM((2, shots * CHUNKS, shots * CHUNKS), BF16),
        ],
        compiler_params=pltpu.CompilerParams(vmem_limit_bytes=limit),
    )(arrived, labels, kernels_rcv)
    returned = lax.all_to_all(back, "shot", split_axis=0, concat_axis=1, tiled=False)
    result = returned.reshape(groups, rcv_dev, 2, CHUNKS, LANES).transpose(0, 2, 1, 3, 4)
    return result.reshape(shot_dev, rcv_dev, samples).astype(F32)


def solution(mesh):
    in_specs = (
        P("shot", "rline", None),
        P(),
        P(),
        P("shot", "rline"),
        P("shot", "rline"),
        P("shot", "rline"),
        P(("shot", "rline")),
    )
    out_specs = P("shot", "rline", None)
    return jax.shard_map(shards, mesh=mesh, in_specs=in_specs, out_specs=out_specs, check_vma=False)
```

time: 521 us -> 83.2 us (0.16)
  the two profiles are of different devices: /device:TPU:1 before, /device:TPU:14 now
where the time goes in v1:
time: 83.2 us; the launch traced here: 82.8 us
  blocking collectives  34.2 us (41%)
  Pallas kernels  25.5 us (31%)
  starting transfers between devices  11.2 us (13%)
  waiting for transfers between devices  5.8 us (7%)
  local copies, waits for them, and re-layouts  3.57 us (4%)
  other arithmetic  2.45 us (3%)
    all_gather x1, blocking collectives, shards(): fold_all = lax.all_gather(fold, 'shot', axis=0, tiled=True)  17.7 us
    all_to_all x1, blocking collectives, shards(): lax.all_to_all(back, 'shot', split_axis=0, concat_axis=1, tiled=False)  16.5 us
    pallas_call x1, Pallas kernels, shards(): pl.pallas_call(receiver_kernel, out_shape=jax.ShapeDtypeStruct((shot_size...  13.6 us
    pallas_call x1, Pallas kernels, shards(): pl.pallas_call(shot_kernel, out_shape=jax.ShapeDtypeStruct((groups, rcv_d...  11.9 us
    ppermute x1, waiting for transfers between devices, shards(): lax.ppermute(head, 'rline', [(i + 1, i) for i in range(ends)])  5.52 us
    all_to_all x1, starting transfers between devices, shards(): lax.all_to_all(sent, 'shot', split_axis=1, concat_axis=0, tiled=False)  5.31 us
    ppermute x1, starting transfers between devices, shards(): lax.ppermute(tail, 'rline', [(i, i + 1) for i in range(ends)])  3.4 us
    ppermute x1, starting transfers between devices, shards(): lax.ppermute(head, 'rline', [(i + 1, i) for i in range(ends)])  2.44 us
  transfers between devices with their start and end apart: 3, of which 2 were waited for; matrix products, arithmetic and copies ran while one was open for 1% of the time, Pallas kernels for 0%

profile of v1, /device:TPU:14, one launch (start us, length us, event | category | flops | bytes accessed | tf_op | source)
XLA Modules:
  0.0 82.8 jit_solution(10481195384776377892)
XLA Ops:
  0.0 0.0 copy-start
  0.0 0.7 broadcast_compare_fusion
  0.7 1.3 %broadcast_select_fusion = bf16[4,96,1024]{2,1,0:T(8,128)(2,1)S(1)} fusion(bf16[4,96,1024]{2,1,0:T(8,128)(2,1)} %param.7, pred[4,96]{1,0:T(4,128)(4,1)S(1)} %broadcast_compare_fusion), kind=kLoop, calls=%fused_computation.3 | loop fusion | flops 393216 | bytes 1573248 | tf_op jit(solution)/shard_map/jit(_where)/select_n | solution.py:206
  2.0 3.4 %collective-permute-start = (bf16[4,7,1024]{2,1,0:T(8,128)(2,1)S(1)}, bf16[4,7,1024]{2,1,0:T(8,128)(2,1)S(1)}, u32[]{:S(2)}, u32[]{:S(2)}) collective-permute-start(bf16[4,7,1024]{2,1,0:T(8,128)(2,1)S(1)} %get-tuple-element.5), channel_id=1, source_target_pairs={{0,1},{1,2},{2,3},{3,4},{4,5},{5,6},{6,7},{7,8},{8,9},{9,10},{10,1... | collective-permute-start | bytes 172040 | tf_op jit(solution)/shard_map/ppermute | solution.py:211
  5.4 2.4 %collective-permute-start.1 = (bf16[4,7,1024]{2,1,0:T(8,128)(2,1)S(1)}, bf16[4,7,1024]{2,1,0:T(8,128)(2,1)S(1)}, u32[]{:S(2)}, u32[]{:S(2)}) collective-permute-start(bf16[4,7,1024]{2,1,0:T(8,128)(2,1)S(1)} %get-tuple-element.6), channel_id=1, source_target_pairs={{1,0},{2,1},{3,2},{4,3},{5,4},{6,5},{7,6},{8,7},{9,8},{10,9},{11,1... | collective-permute-start | bytes 172040 | tf_op jit(solution)/shard_map/ppermute | solution.py:213
  7.9 0.0 copy-done
  7.9 0.3 collective-permute-done
  8.2 5.5 %collective-permute-done.1 = bf16[4,7,1024]{2,1,0:T(8,128)(2,1)S(1)} collective-permute-done((bf16[4,7,1024]{2,1,0:T(8,128)(2,1)S(1)}, bf16[4,7,1024]{2,1,0:T(8,128)(2,1)S(1)}, u32[]{:S(2)}, u32[]{:S(2)}) %collective-permute-start.1) | collective-permute-done | bytes 57376 | tf_op jit(solution)/shard_map/ppermute | solution.py:213
  13.7 0.3 pad_maximum_fusion
  13.9 0.4 reshape.50
  14.4 0.2 copy.36
  14.5 11.9 %shard_map.55 = bf16[2,96,16,128]{3,2,1,0:T(8,128)(2,1)S(1)} custom-call(bf16[2,110,16,128]{3,2,1,0:T(8,128)(2,1)S(1)} %bitcast.28, bf16[4,15,31]{2,1,0:T(8,128)(2,1)S(1)} %copy.26.kernel_ref), custom_call_target="tpu_custom_call" | custom-call | tf_op jit(solution)/shard_map/pallas_call | solution.py:221
  26.4 0.0 copy-start.1
  26.5 0.0 copy-start.2
  26.5 1.0 %copy.27 = bf16[1,2,8,12,16,128]{5,4,3,1,0,2:T(8,128)(2,1)} copy(bf16[1,2,8,12,16,128]{5,4,3,2,1,0:T(8,128)(2,1)S(1)} %bitcast.31) | data formatting | bytes 1572864 | tf_op jit(solution)/shard_map/broadcast_in_dim;reshape | solution.py:238
  27.5 5.3 %all-to-all-start = ((bf16[1,2,8,12,16,128]{5,4,3,1,0,2:T(8,128)(2,1)}), bf16[1,2,8,12,16,128]{5,4,3,1,0,2:T(8,128)(2,1)S(1)}, u32[]{:S(2)}, u32[]{:S(2)}) async-start(bf16[1,2,8,12,16,128]{5,4,3,1,0,2:T(8,128)(2,1)} %copy.27), calls=%async_computation | async-start | bytes 1572864 | tf_op jit(solution)/shard_map/all_to_all | solution.py:238
  32.8 0.0 copy-done.1
  32.8 0.0 copy-done.2
  32.8 17.7 %all-gather = s32[8,4,96]{2,1,0:T(4,128)S(1)} all-gather(s32[1,4,96]{2,1,0:T(4,128)S(1)} %bitcast.34), channel_id=1, replica_groups=mesh['shot'=8,'rline'=16] {'shot'}, dimensions={0}, use_global_device_ids=true | all-gather | bytes 13824 | tf_op jit(solution)/shard_map/all_gather | solution.py:205
  50.6 0.1 select_bitcast_fusion
  50.7 0.1 copy.28
  50.7 0.1 add.33
  50.8 0.1 add.30
  50.9 0.1 add.36
  51.1 0.0 all-to-all-done
  51.1 13.6 %shard_map.56 = bf16[8,2,12,16,128]{4,3,2,1,0:T(8,128)(2,1)S(1)} custom-call(bf16[8,2,12,16,128]{4,3,2,1,0:T(8,128)(2,1)S(1)} %bitcast.29, s32[12,1,256]{2,1,0:T(1,128)S(1)} %broadcast_add_fusion.fold_ref, bf16[4,15,31]{2,1,0:T(8,128)(2,1)S(1)} %copy.30.kernel_ref), custom_call_target="tpu_custom_call" | custom-call | tf_op jit(solution)/shard_map/pallas_call | solution.py:239
  64.7 16.5 %all_to_all.27 = bf16[8,2,1,12,16,128]{5,4,3,1,2,0:T(8,128)(2,1)S(1)} all-to-all(bf16[8,2,1,12,16,128]{5,4,3,1,2,0:T(8,128)(2,1)S(1)} %bitcast.30), channel_id=1, replica_groups=mesh['shot'=8,'rline'=16] {'shot'}, dimensions={0} | all-to-all | bytes 1572864 | tf_op jit(solution)/shard_map/all_to_all | solution.py:252
  81.2 0.2 bitcast_convert_fusion
  81.4 0.1 copy.33
  81.5 1.4 %reshape.52 = f32[4,96,1024]{2,1,0:T(8,128)} reshape(f32[2,2,96,8,128]{4,3,2,1,0:T(8,128)S(1)} %copy.33) | data formatting | bytes 3145728 | tf_op jit(solution)/shard_map/convert_element_type | solution.py:254
  (5 shorter events, 0.0 us)
Async XLA Ops:
  0.0 7.9 %copy-start = (bf16[4,15,31]{2,0,1:T(4,128)(2,1)S(1)}, bf16[4,15,31]{2,0,1:T(4,128)(2,1)}, u32[]{:S(2)}) copy-start(bf16[4,15,31]{2,0,1:T(4,128)(2,1)} %param.8) | copy-start | bytes 11164
  2.0 6.2 %collective-permute-start = (bf16[4,7,1024]{2,1,0:T(8,128)(2,1)S(1)}, bf16[4,7,1024]{2,1,0:T(8,128)(2,1)S(1)}, u32[]{:S(2)}, u32[]{:S(2)}) collective-permute-start(bf16[4,7,1024]{2,1,0:T(8,128)(2,1)S(1)} %get-tuple-element.5), channel_id=1, source_target_pairs={{0,1},{1,2},{2,3},{3,4},{4,5},{5,6},{6,7},{7,8},{8,9},{9,10},{10,1... | collective-permute-start | bytes 172040 | tf_op jit(solution)/shard_map/ppermute | solution.py:211
  5.4 8.3 %collective-permute-start.1 = (bf16[4,7,1024]{2,1,0:T(8,128)(2,1)S(1)}, bf16[4,7,1024]{2,1,0:T(8,128)(2,1)S(1)}, u32[]{:S(2)}, u32[]{:S(2)}) collective-permute-start(bf16[4,7,1024]{2,1,0:T(8,128)(2,1)S(1)} %get-tuple-element.6), channel_id=1, source_target_pairs={{1,0},{2,1},{3,2},{4,3},{5,4},{6,5},{7,6},{8,7},{9,8},{10,9},{11,1... | collective-permute-start | bytes 172040 | tf_op jit(solution)/shard_map/ppermute | solution.py:213
  26.4 6.4 %copy-start.1 = (bf16[4,15,31]{2,0,1:T(4,128)(2,1)S(1)}, bf16[4,15,31]{2,0,1:T(4,128)(2,1)}, u32[]{:S(2)}) copy-start(bf16[4,15,31]{2,0,1:T(4,128)(2,1)} %param.9) | copy-start | bytes 11164
  26.5 6.4 %copy-start.2 = (s32[4,96]{1,0:T(4,128)S(1)}, s32[4,96]{1,0:T(4,128)}, u32[]{:S(2)}) copy-start(s32[4,96]{1,0:T(4,128)} %param.11) | copy-start | bytes 4612
  27.5 23.6 %all-to-all-start = ((bf16[1,2,8,12,16,128]{5,4,3,1,0,2:T(8,128)(2,1)}), bf16[1,2,8,12,16,128]{5,4,3,1,0,2:T(8,128)(2,1)S(1)}, u32[]{:S(2)}, u32[]{:S(2)}) async-start(bf16[1,2,8,12,16,128]{5,4,3,1,0,2:T(8,128)(2,1)} %copy.27), calls=%async_computation | async-start | bytes 1572864 | tf_op jit(solution)/shard_map/all_to_all | solution.py:238

commit v2 on v1

v2 whole, which is shorter than its diff:
```python
import functools

import jax
import jax.numpy as jnp
from jax import lax
from jax.experimental import pallas as pl
from jax.experimental.pallas import tpu as pltpu
from jax.sharding import PartitionSpec as P

LANES = 128
CHUNKS = 8
BF16 = jnp.bfloat16
F32 = jnp.float32
RIM = 7
MESH = pl.DeviceIdType.MESH


def lane_index(shape):
    return lax.broadcasted_iota(jnp.int32, shape, len(shape) - 1)


def build_table(kernel_ref, table_ref):
    taps = kernel_ref.shape[2]
    tap = lax.broadcasted_iota(jnp.int32, (taps, LANES), 0)
    lane = lax.broadcasted_iota(jnp.int32, (taps, LANES), 1)
    place_low = (lane == LANES - 1 - tap).astype(BF16)
    place_high = (lane == LANES // 2 - 1 - tap).astype(BF16)
    even = (lane_index((64, LANES)) // 32) % 2 == 0
    for half in range(2):
        base = jnp.dot(kernel_ref[2 * half], place_low, preferred_element_type=F32) + jnp.dot(
            kernel_ref[2 * half + 1], place_high, preferred_element_type=F32
        )
        before = jnp.zeros((64, LANES), F32)
        for step in range(16):
            if step < 15:
                row = jnp.broadcast_to(base[step : step + 1], (64, LANES))
                here = pltpu.roll(row, 0, 1, stride=1, stride_axis=0)
            else:
                here = jnp.zeros((64, LANES), F32)
            block = jnp.where(even, here, pltpu.roll(before, 32, 1))
            table_ref[step * 64 : (step + 1) * 64, half * LANES : (half + 1) * LANES] = block.astype(BF16)
            before = here


def windows(first, second):
    shape = first.shape
    lane = lane_index(shape)
    chunk = lax.broadcasted_iota(jnp.int32, shape, 1)
    low = lane < 64

    def both(x):
        left = jnp.where(chunk == 0, 0.0, pltpu.roll(x, 1, 1))
        right = jnp.where(chunk == CHUNKS - 1, 0.0, pltpu.roll(x, CHUNKS - 1, 1))
        early = pltpu.roll(jnp.where(lane < 112, x, left), 16, 2)
        late = pltpu.roll(jnp.where(lane >= 16, x, right), 112, 2)
        return early, late

    early_a, late_a = both(first)
    early_b, late_b = both(second)
    return (
        jnp.where(low, early_a, pltpu.roll(early_b, 64, 2)),
        jnp.where(low, late_a, pltpu.roll(late_b, 64, 2)),
        jnp.where(low, pltpu.roll(early_a, 64, 2), early_b),
        jnp.where(low, pltpu.roll(late_a, 64, 2), late_b),
    )


def fan_terms(window_ref, table_ref, start, pairs):
    rows = pairs * 16
    left = jnp.concatenate(
        [
            jnp.concatenate(
                [window_ref[quarter, pl.ds(start + step, pairs)].reshape(rows, LANES) for step in range(8)],
                axis=1,
            )
            for quarter in range(4)
        ],
        axis=0,
    )
    coherent = jnp.dot(left, table_ref[...], preferred_element_type=F32)
    squares, cubes = [], []
    for quarter in range(4):
        part = coherent[quarter * rows : (quarter + 1) * rows]
        one, two = part[:, :LANES], part[:, LANES:]
        one_sq, two_sq = one * one, two * two
        squares.append(one_sq + two_sq)
        cubes.append(one_sq * one + two_sq * two)
    lane = lane_index((rows, LANES))
    low = lane < 64
    even = (lane // 32) % 2 == 0

    def merged(s):
        s02, s20 = jnp.where(low, s[0], s[2]), jnp.where(low, s[2], s[0])
        s13, s31 = jnp.where(low, s[1], s[3]), jnp.where(low, s[3], s[1])
        a = jnp.where(even, s02, s13) + pltpu.roll(jnp.where(even, s20, s31), 64, 1)
        b = jnp.where(even, s13, s02) + pltpu.roll(jnp.where(even, s31, s20), 64, 1)
        return a, b

    square_a, square_b = merged(squares)
    cube_a, cube_b = merged(cubes)
    term_a = cube_a / (square_a + 1.0)
    term_b = cube_b / (square_b + 1.0)
    return (
        jnp.where(even, term_a, pltpu.roll(term_b, 32, 1)),
        jnp.where(even, pltpu.roll(term_b, 96, 1), term_a),
    )


def fill_windows(source, window_ref, first, pairs):
    x = source.reshape(pairs, 2, 2, CHUNKS, LANES)
    one = x[:, 0].reshape(pairs * 2, CHUNKS, LANES)
    two = x[:, 1].reshape(pairs * 2, CHUNKS, LANES)
    for quarter, tile in enumerate(windows(one, two)):
        window_ref[quarter, pl.ds(first, pairs)] = tile.reshape(pairs, 16, LANES).astype(BF16)


def interleaved(even, odd, pairs):
    return jnp.stack(
        [even.reshape(pairs, 16, LANES), odd.reshape(pairs, 16, LANES)], axis=1
    ).reshape(2 * pairs, 16, LANES)


def survey_kernel(
    shot_size,
    rline_size,
    x_ref,
    fold_ref,
    shot_taps_ref,
    rcv_taps_ref,
    out_ref,
    padded_ref,
    window_ref,
    shot_table_ref,
    rcv_table_ref,
    fold_own_ref,
    fold_ref_all,
    label_ref,
    pick_ref,
    sent_ref,
    held_ref,
    stack_ref,
    rcv_window_ref,
    back_ref,
    halo_send,
    halo_recv,
    fold_send,
    fold_recv,
    out_send,
    out_recv,
    own_sem,
    back_send,
    back_recv,
    back_own,
):
    groups, receivers = x_ref.shape[0], x_ref.shape[1]
    share = receivers // shot_size
    peers = shot_size - 1
    shots = shot_size * groups * 2
    rows = shots * CHUNKS
    me = lax.axis_index("shot")
    line = lax.axis_index("rline")
    right, left = lax.rem(line + 1, rline_size), lax.rem(line + rline_size - 1, rline_size)

    def peer(step):
        return lax.rem(me + 1 + step, shot_size)

    def source(step):
        return lax.rem(me + shot_size - 1 - step, shot_size)

    barrier = pltpu.get_barrier_semaphore()
    for step in range(peers):
        pl.semaphore_signal(barrier, inc=1, device_id={"shot": peer(step)}, device_id_type=MESH)
    for side in (left, right):
        pl.semaphore_signal(barrier, inc=1, device_id={"rline": side}, device_id_type=MESH)
    pl.semaphore_wait(barrier, peers + 2)

    def halo(side):
        begin = receivers - RIM if side == 0 else 0
        land = 0 if side == 0 else RIM + receivers
        return pltpu.make_async_remote_copy(
            src_ref=x_ref.at[:, pl.ds(begin, RIM)],
            dst_ref=padded_ref.at[:, pl.ds(land, RIM)],
            send_sem=halo_send.at[side],
            recv_sem=halo_recv.at[side],
            device_id={"rline": right if side == 0 else left},
            device_id_type=MESH,
        )

    def fold_copy(step, slot):
        return pltpu.make_async_remote_copy(
            src_ref=fold_own_ref,
            dst_ref=fold_ref_all.at[slot],
            send_sem=fold_send.at[step],
            recv_sem=fold_recv.at[step],
            device_id={"shot": peer(step)},
            device_id_type=MESH,
        )

    for side in range(2):
        halo(side).start()
    fold_own_ref[...] = jnp.full(fold_own_ref.shape, -1, jnp.int32)
    fold_own_ref[0 : fold_ref.shape[0], 0:receivers] = fold_ref[...]
    for step in range(peers):
        fold_copy(step, me).start()
    fold_ref_all[me] = fold_own_ref[...]

    for g in range(groups):
        padded_ref[g, RIM : RIM + receivers] = x_ref[g]
    build_table(shot_taps_ref, shot_table_ref)
    build_table(rcv_taps_ref, rcv_table_ref)

    for side in range(2):
        halo(side).wait_recv()
    keep_left = (line > 0).astype(F32)
    keep_right = (line < rline_size - 1).astype(F32)
    for g in range(groups):
        padded_ref[g, 0:RIM] = (padded_ref[g, 0:RIM].astype(F32) * keep_left).astype(BF16)
        tail = pl.ds(RIM + receivers, RIM)
        padded_ref[g, tail] = (padded_ref[g, tail].astype(F32) * keep_right).astype(BF16)

    step_pairs = 5
    for g in range(groups):

        @pl.loop(0, (receivers + 2 * RIM) // (2 * step_pairs))
        def _(i):
            x = padded_ref[g, pl.ds(i * 2 * step_pairs, 2 * step_pairs)].astype(F32)
            fill_windows(x, window_ref.at[g], i * step_pairs, step_pairs)

    def out_copy(step, target, slot):
        return pltpu.make_async_remote_copy(
            src_ref=sent_ref.at[target],
            dst_ref=held_ref.at[slot],
            send_sem=out_send.at[step],
            recv_sem=out_recv.at[step],
            device_id={"shot": peer(step)},
            device_id_type=MESH,
        )

    pairs = share // 2

    @pl.loop(0, shot_size)
    def _(step):
        target = peer(step)
        for g in range(groups):
            even, odd = fan_terms(window_ref.at[g], shot_table_ref, target * pairs, pairs)
            centre = padded_ref[g, pl.ds(target * share + RIM, share)].astype(F32)
            sent_ref[target, g] = (centre - interleaved(even, odd, pairs)).astype(BF16)

        @pl.when(step < peers)
        def _():
            out_copy(step, target, me).start()

        @pl.when(step == peers)
        def _():
            pltpu.make_async_copy(sent_ref.at[me], held_ref.at[me], own_sem).start()

    for step in range(peers):
        fold_copy(step, source(step)).wait_recv()
    folds = fold_ref_all[...].reshape(shot_size * 8, LANES).astype(F32)
    take = lax.broadcasted_iota(jnp.int32, (16, LANES), 1) == (
        me * share + lax.broadcasted_iota(jnp.int32, (16, LANES), 0)
    )
    mine = lax.dot_general(
        take.astype(F32), folds, (((1,), (1,)), ((), ())), preferred_element_type=F32
    )
    entry = lax.broadcasted_iota(jnp.int32, (shot_size * 8, rows), 0)
    shot = lax.broadcasted_iota(jnp.int32, (shot_size * 8, rows), 1) // CHUNKS
    per = groups * 2
    spread = ((entry // 8) * per + entry % 8 == shot) & (entry % 8 < per)
    lane = lax.broadcasted_iota(jnp.int32, (16, rows), 1)
    labels = jnp.dot(mine, spread.astype(F32), preferred_element_type=F32)
    labels = jnp.where(labels >= 0.0, labels * CHUNKS + (lane % CHUNKS).astype(F32), -1.0)
    place = lax.broadcasted_iota(jnp.int32, (rows, rows), 0).astype(F32)
    for k in range(share):
        label_ref[k] = labels[k : k + 1]

    @pl.loop(0, share)
    def _(k):
        pick_ref[k] = jnp.where(label_ref[k] == place, 1.0, 0.0).astype(BF16)

    stack_ref[0:RIM] = jnp.zeros((RIM, 16, LANES), F32)
    stack_ref[RIM + shots : 16 + shots] = jnp.zeros((16 - RIM, 16, LANES), F32)
    pltpu.make_async_copy(sent_ref.at[me], held_ref.at[me], own_sem).wait()
    for step in range(peers):
        out_copy(step, peer(step), source(step)).wait_recv()

    def back_copy(g, step, owner):
        return pltpu.make_async_remote_copy(
            src_ref=back_ref.at[g, peer(step)],
            dst_ref=out_ref.at[:, pl.ds(owner * share + 2 * g, 2)],
            send_sem=back_send.at[g, step],
            recv_sem=back_recv.at[g, step],
            device_id={"shot": peer(step)},
            device_id_type=MESH,
        )

    def back_local(g):
        return pltpu.make_async_copy(
            back_ref.at[g, me], out_ref.at[:, pl.ds(me * share + 2 * g, 2)], back_own.at[g]
        )

    @pl.loop(0, pairs)
    def _(g):
        gains = []
        for side in range(2):
            k = 2 * g + side
            live = jnp.sum((label_ref[k] >= 0.0).astype(F32), axis=1, keepdims=True) / CHUNKS
            gains.append(jnp.sqrt(shots / live))
            x = held_ref[:, :, k].reshape(rows, LANES)
            stack = jnp.dot(pick_ref[k], x, preferred_element_type=F32).reshape(shots, CHUNKS, LANES)
            stack_ref[RIM : RIM + shots, side * CHUNKS : (side + 1) * CHUNKS] = stack

        @pl.loop(0, 4)
        def _(i):
            fill_windows(stack_ref[pl.ds(i * 12, 12)], rcv_window_ref, i * 6, 6)

        value = []
        count = shots // 4
        for half in range(2):
            even, odd = fan_terms(rcv_window_ref, rcv_table_ref, half * count, count)
            begin = RIM + 2 * half * count
            value.append(stack_ref[begin : begin + 2 * count] - interleaved(even, odd, count))
        value = jnp.concatenate(value, axis=0)
        for side in range(2):
            own = value[:, side * CHUNKS : (side + 1) * CHUNKS].reshape(rows, LANES) * gains[side]
            back = lax.dot_general(
                pick_ref[2 * g + side], own.astype(BF16), (((0,), (0,)), ((), ())), preferred_element_type=F32
            )
            back_ref[g, :, :, side] = back.astype(BF16).reshape(shot_size, groups, 16, LANES)
        for step in range(peers):
            back_copy(g, step, me).start()
        back_local(g).start()

    for side in range(2):
        halo(side).wait_send()
    for step in range(peers):
        fold_copy(step, me).wait_send()
        out_copy(step, peer(step), me).wait_send()

    @pl.loop(0, pairs)
    def _(g):
        back_local(g).wait()
        for step in range(peers):
            back_copy(g, step, me).wait_send()
            back_copy(g, step, source(step)).wait_recv()


def vmem():
    return pl.BlockSpec(memory_space=pltpu.VMEM)


def shards(traces, kernels_shot, kernels_rcv, dest, gather, fold, counts):
    shot_dev, rcv_dev, samples = traces.shape
    shot_size = lax.axis_size("shot")
    rline_size = lax.axis_size("rline")
    shots = shot_dev * shot_size
    share = rcv_dev // shot_size
    rows = shots * CHUNKS
    groups = shot_dev // 2
    peers = shot_size - 1
    pairs = share // 2
    span = rcv_dev + 2 * RIM

    cleaned = jnp.where((dest >= 0)[..., None], traces, jnp.zeros_like(traces))
    x = cleaned.reshape(groups, 2, rcv_dev, CHUNKS, LANES).transpose(0, 2, 1, 3, 4)
    x = x.reshape(groups, rcv_dev, 16, LANES)
    dma = pltpu.SemaphoreType.DMA
    returned = pl.pallas_call(
        functools.partial(survey_kernel, shot_size, rline_size),
        out_shape=jax.ShapeDtypeStruct((groups, rcv_dev, 16, LANES), BF16),
        in_specs=[vmem()] * 4,
        out_specs=vmem(),
        scratch_shapes=[
            pltpu.VMEM((groups, span, 16, LANES), BF16),
            pltpu.VMEM((groups, 4, span // 2, 16, LANES), BF16),
            pltpu.VMEM((1024, 256), BF16),
            pltpu.VMEM((1024, 256), BF16),
            pltpu.VMEM((8, LANES), jnp.int32),
            pltpu.VMEM((shot_size, 8, LANES), jnp.int32),
            pltpu.VMEM((share, 1, rows), F32),
            pltpu.VMEM((share, rows, rows), BF16),
            pltpu.VMEM((shot_size, groups, share, 16, LANES), BF16),
            pltpu.VMEM((shot_size, groups, share, 16, LANES), BF16),
            pltpu.VMEM((shots + 16, 16, LANES), F32),
            pltpu.VMEM((4, shots // 2 + 8, 16, LANES), BF16),
            pltpu.VMEM((pairs, shot_size, groups, 2, 16, LANES), BF16),
            dma((2,)),
            dma((2,)),
            dma((peers,)),
            dma((peers,)),
            dma((peers,)),
            dma((peers,)),
            dma,
            dma((pairs, peers)),
            dma((pairs, peers)),
            dma((pairs,)),
        ],
        compiler_params=pltpu.CompilerParams(
            vmem_limit_bytes=48 << 20, collective_id=0, has_side_effects=True
        ),
        cost_estimate=pl.CostEstimate(flops=7 * 10**9, bytes_accessed=4 * 10**6, transcendentals=0),
    )(x, fold, kernels_shot, kernels_rcv)
    result = returned.reshape(groups, rcv_dev, 2, CHUNKS, LANES).transpose(0, 2, 1, 3, 4)
    return result.reshape(shot_dev, rcv_dev, samples).astype(F32)


def solution(mesh):
    in_specs = (
        P("shot", "rline", None),
        P(),
        P(),
        P("shot", "rline"),
        P("shot", "rline"),
        P("shot", "rline"),
        P(("shot", "rline")),
    )
    out_specs = P("shot", "rline", None)
    return jax.shard_map(shards, mesh=mesh, in_specs=in_specs, out_specs=out_specs, check_vma=False)
```

time: 83.2 us -> 52.2 us (0.63)
  the two profiles are of different devices: /device:TPU:14 before, /device:TPU:1 now
where the time goes in v2:
time: 52.2 us; the launch traced here: 51.9 us
  Pallas kernels  46.2 us (89%)
  local copies, waits for them, and re-layouts  3.58 us (7%)
  other arithmetic  2.06 us (4%)
    pallas_call x1, Pallas kernels, shards(): pl.pallas_call(functools.partial(survey_kernel, shot_size, rline_size), o...  46.2 us
    unnamed x5, local copies, waits for them, and re-layouts  1.96 us
    convert_element_type x2, local copies, waits for them, and re-layouts, shards(): return result.reshape(shot_dev, rcv_dev, samples).astype(F32)  1.48 us
    select_n x1, other arithmetic, shards(): cleaned = jnp.where((dest >= 0)[..., None], traces, jnp.zeros_like(traces))  1.25 us

profile of v2, /device:TPU:1, one launch (start us, length us, event | category | flops | bytes accessed | tf_op | source)
XLA Modules:
  0.0 51.9 jit_solution(14636730764441639957)
XLA Ops:
  0.0 0.7 %broadcast_compare_fusion = pred[4,96]{1,0:T(4,128)(4,1)S(1)} fusion(s32[4,96]{1,0:T(4,128)} %param.10), kind=kLoop, calls=%fused_computation.3 | loop fusion | flops 384 | bytes 1920 | tf_op jit(solution)/shard_map/ge | solution.py:364
  0.7 0.7 %copy.7.shot_taps_ref = bf16[4,15,31]{2,1,0:T(8,128)(2,1)S(1)} copy(bf16[4,15,31]{2,0,1:T(4,128)(2,1)} %param.8) | data formatting | bytes 7440 | tf_op args[1]
  1.4 0.7 %copy.8.rcv_taps_ref = bf16[4,15,31]{2,1,0:T(8,128)(2,1)S(1)} copy(bf16[4,15,31]{2,0,1:T(4,128)(2,1)} %param.9) | data formatting | bytes 7440 | tf_op args[2]
  2.1 1.3 %broadcast_select_fusion = bf16[4,96,1024]{2,1,0:T(8,128)(2,1)S(1)} fusion(bf16[4,96,1024]{2,1,0:T(8,128)(2,1)} %param.7, pred[4,96]{1,0:T(4,128)(4,1)S(1)} %broadcast_compare_fusion), kind=kLoop, calls=%fused_computation.2 | loop fusion | flops 393216 | bytes 1573248 | tf_op jit(solution)/shard_map/jit(_where)/select_n | solution.py:364
  3.4 0.0 copy-start
  3.4 0.2 copy.10
  3.6 0.1 copy.12
  3.7 0.3 copy-done
  4.1 46.2 %shard_map.55 = bf16[2,96,16,128]{3,2,1,0:T(8,128)(2,1)S(1)} custom-call(bf16[2,96,16,128]{3,2,1,0:T(8,128)(2,1)S(1)} %bitcast.16, s32[4,96]{1,0:T(4,128)S(1)} %copy-done, bf16[4,15,31]{2,1,0:T(8,128)(2,1)S(1)} %copy.7.shot_taps_ref, bf16[4,15,31]{2,1,0:T(8,128)(2,1)S(1)} %copy.8.rcv_taps_ref), custom_call_target="tpu_custom_call" | custom-call | flops 7000000000 | bytes 4000000 | tf_op jit(solution)/shard_map/pallas_call | solution.py:368
  50.3 0.1 convert_bitcast_fusion
  50.4 0.1 copy.9
  50.5 1.4 %reshape.15 = f32[4,96,1024]{2,1,0:T(8,128)} reshape(f32[2,2,96,8,128]{4,3,2,1,0:T(8,128)S(1)} %copy.9) | data formatting | bytes 3145728 | tf_op jit(solution)/shard_map/convert_element_type | solution.py:404
Async XLA Ops:
  3.4 0.7 %copy-start = (s32[4,96]{1,0:T(4,128)S(1)}, s32[4,96]{1,0:T(4,128)}, u32[]{:S(2)}) copy-start(s32[4,96]{1,0:T(4,128)} %fold_ref.1) | copy-start | bytes 4612

commit v3 on v2

v3 whole, which is shorter than its diff:
```python
import functools

import jax
import jax.numpy as jnp
from jax import lax
from jax.experimental import pallas as pl
from jax.experimental.pallas import tpu as pltpu
from jax.sharding import PartitionSpec as P

LANES = 128
CHUNKS = 8
BF16 = jnp.bfloat16
F32 = jnp.float32
RIM = 7
PIECES = 3
MESH = pl.DeviceIdType.MESH


def lane_index(shape):
    return lax.broadcasted_iota(jnp.int32, shape, len(shape) - 1)


def build_table(kernel_ref, table_ref):
    taps = kernel_ref.shape[2]
    tap = lax.broadcasted_iota(jnp.int32, (taps, LANES), 0)
    lane = lax.broadcasted_iota(jnp.int32, (taps, LANES), 1)
    place_low = (lane == LANES - 1 - tap).astype(BF16)
    place_high = (lane == LANES // 2 - 1 - tap).astype(BF16)
    even = (lane_index((64, LANES)) // 32) % 2 == 0
    for half in range(2):
        base = jnp.dot(kernel_ref[2 * half], place_low, preferred_element_type=F32) + jnp.dot(
            kernel_ref[2 * half + 1], place_high, preferred_element_type=F32
        )
        before = jnp.zeros((64, LANES), F32)
        columns = slice(half * LANES, (half + 1) * LANES)
        for step in range(16):
            if step < 15:
                row = jnp.broadcast_to(base[step : step + 1], (64, LANES))
                here = pltpu.roll(row, 0, 1, stride=1, stride_axis=0)
            else:
                here = jnp.zeros((64, LANES), F32)
            block = jnp.where(even, here, pltpu.roll(before, 32, 1)).astype(BF16)
            table_ref[0, step * 64 : (step + 1) * 64, columns] = block
            other = step + 1 if step % 2 == 0 else step - 1
            table_ref[1, other * 64 : (other + 1) * 64, columns] = block
            before = here


def fill_windows(source_ref, window_ref, first, pairs):
    rows = pairs * 32
    begin = first * 32 + 8
    shape = (pairs, 2, 16, LANES)
    lane = lane_index(shape)
    chunk = lax.broadcasted_iota(jnp.int32, shape, 2) % CHUNKS
    own = source_ref[pl.ds(begin, rows)].reshape(shape)
    left = source_ref[pl.ds(begin - 1, rows)].reshape(shape)
    right = source_ref[pl.ds(begin + 1, rows)].reshape(shape)
    early = jnp.where(lane < 112, own, jnp.where(chunk == 0, 0.0, left))
    late = jnp.where(lane >= 16, own, jnp.where(chunk == CHUNKS - 1, 0.0, right))
    low = lane_index((pairs * 16, LANES)) < 64

    def turned(x, shift):
        return pltpu.roll(x.reshape(pairs * 16, LANES), shift, 1)

    early_a, early_b = turned(early[:, 0], 16), turned(early[:, 1], 80)
    late_a, late_b = turned(late[:, 0], 112), turned(late[:, 1], 48)
    tiles = (
        jnp.where(low, early_a, early_b),
        jnp.where(low, late_a, late_b),
        jnp.where(low, early_b, early_a),
        jnp.where(low, late_b, late_a),
    )
    for quarter, tile in enumerate(tiles):
        window_ref[quarter, pl.ds(first, pairs)] = tile.reshape(pairs, 16, LANES).astype(BF16)


def fan_terms(blocks, table_ref, pairs):
    rows = pairs * 16
    total = len(blocks) * rows
    parts = []
    for half in range(2):
        left = jnp.concatenate(
            [
                jnp.concatenate(
                    [ref[quarter, pl.ds(first + step, pairs)].reshape(rows, LANES) for step in range(8)],
                    axis=1,
                )
                for quarter in (2 * half, 2 * half + 1)
                for ref, first in blocks
            ],
            axis=0,
        )
        coherent = jnp.dot(left, table_ref[half], preferred_element_type=F32)
        parts += [coherent[:total], coherent[total:]]
    squares, cubes = [], []
    for part in parts:
        one, two = part[:, :LANES], part[:, LANES:]
        one_sq, two_sq = one * one, two * two
        squares.append(one_sq + two_sq)
        cubes.append(one_sq * one + two_sq * two)
    lane = lane_index((total, LANES))
    low = lane < 64
    even = (lane // 32) % 2 == 0

    def merged(s):
        s02, s20 = jnp.where(low, s[0], s[2]), jnp.where(low, s[2], s[0])
        s13, s31 = jnp.where(low, s[1], s[3]), jnp.where(low, s[3], s[1])
        a = jnp.where(even, s02, s13) + pltpu.roll(jnp.where(even, s20, s31), 64, 1)
        b = jnp.where(even, s13, s02) + pltpu.roll(jnp.where(even, s31, s20), 64, 1)
        return a, b

    square_a, square_b = merged(squares)
    cube_a, cube_b = merged(cubes)
    term_a = cube_a / (square_a + 1.0)
    term_b = cube_b / (square_b + 1.0)
    first_trace = jnp.where(even, term_a, pltpu.roll(term_b, 32, 1))
    second_trace = jnp.where(even, pltpu.roll(term_b, 96, 1), term_a)
    shape = (len(blocks) * pairs, 16, LANES)
    both = jnp.stack([first_trace.reshape(shape), second_trace.reshape(shape)], axis=1)
    both = both.reshape(len(blocks), 2 * pairs, 16, LANES)
    return [both[i] for i in range(len(blocks))]


def survey_kernel(
    shot_size,
    rline_size,
    traces_hbm,
    dest_hbm,
    fold_hbm,
    shot_taps_hbm,
    rcv_taps_hbm,
    out_ref,
    traces_ref,
    dest_ref,
    fold_ref,
    shot_taps_ref,
    rcv_taps_ref,
    alive_ref,
    mask_ref,
    plain_ref,
    window_ref,
    shot_table_ref,
    rcv_table_ref,
    halo_out_ref,
    halo_in_ref,
    fold_own_ref,
    fold_all_ref,
    gain_ref,
    pick_ref,
    unpick_ref,
    sent_ref,
    held_ref,
    stack_ref,
    rcv_window_ref,
    back_ref,
    load_sem,
    halo_send,
    halo_recv,
    fold_send,
    fold_recv,
    out_send,
    out_recv,
    back_send,
    back_recv,
):
    shot_dev, receivers = traces_ref.shape[0], traces_ref.shape[1]
    groups = shot_dev // 2
    share = receivers // shot_size
    peers = shot_size - 1
    shots = shot_size * shot_dev
    rows = shots * CHUNKS
    me = lax.axis_index("shot")
    line = lax.axis_index("rline")
    right, left = lax.rem(line + 1, rline_size), lax.rem(line + rline_size - 1, rline_size)

    def peer(step):
        return lax.rem(me + 1 + step, shot_size)

    def source(step):
        return lax.rem(me + shot_size - 1 - step, shot_size)

    loads = [
        pltpu.make_async_copy(a, b, load_sem.at[i])
        for i, (a, b) in enumerate(
            [
                (shot_taps_hbm, shot_taps_ref),
                (rcv_taps_hbm, rcv_taps_ref),
                (dest_hbm, dest_ref),
                (fold_hbm, fold_ref),
                (traces_hbm, traces_ref),
            ]
        )
    ]
    for load in loads:
        load.start()
    barrier = pltpu.get_barrier_semaphore()
    for step in range(peers):
        pl.semaphore_signal(barrier, inc=1, device_id={"shot": peer(step)}, device_id_type=MESH)
    for side in (left, right):
        pl.semaphore_signal(barrier, inc=1, device_id={"rline": side}, device_id_type=MESH)

    alive_ref[...] = jnp.zeros(alive_ref.shape, F32)
    fold_own_ref[...] = jnp.full(fold_own_ref.shape, -1, jnp.int32)
    loads[0].wait()
    build_table(shot_taps_ref, shot_table_ref)
    loads[2].wait()
    alive_ref[0:shot_dev, 0:receivers] = (dest_ref[...] >= 0).astype(F32)
    pick_shot = lax.broadcasted_iota(jnp.int32, (8, shot_dev * LANES), 0) == (
        lax.broadcasted_iota(jnp.int32, (8, shot_dev * LANES), 1) // LANES
    )
    mask_ref[...] = lax.dot_general(
        alive_ref[...], pick_shot.astype(F32), (((0,), (0,)), ((), ())), preferred_element_type=F32
    )
    loads[4].wait()
    for s in range(shot_dev):

        @pl.loop(0, receivers // 16)
        def _(i):
            x = traces_ref[s, pl.ds(i * 16, 16)].astype(F32)
            for half in range(2):
                mask = mask_ref[pl.ds(i * 16 + half * 8, 8), s * LANES : (s + 1) * LANES]
                begin = (i * 16 + half * 8 + RIM) * 16 + 8 + (s % 2) * CHUNKS
                for c in range(CHUNKS):
                    piece = x[half * 8 : half * 8 + 8, c * LANES : (c + 1) * LANES]
                    plain_ref[s // 2, pl.ds(begin + c, 8, stride=16)] = piece * mask

    for g in range(groups):
        for side, begin in enumerate((receivers - RIM, 0)):
            edge = plain_ref[g, (RIM + begin) * 16 + 8 : (2 * RIM + begin) * 16 + 8]
            halo_out_ref[side, g] = edge.astype(BF16).reshape(RIM, 16, LANES)
    loads[3].wait()
    fold_own_ref[0:shot_dev, 0:receivers] = fold_ref[...]

    step_pairs = 5
    span_pairs = (receivers + 2 * RIM) // 2
    for g in range(groups):

        @pl.loop(1, span_pairs // step_pairs - 1)
        def _(i):
            fill_windows(plain_ref.at[g], window_ref.at[g], i * step_pairs, step_pairs)

    def halo(side):
        return pltpu.make_async_remote_copy(
            src_ref=halo_out_ref.at[side],
            dst_ref=halo_in_ref.at[side],
            send_sem=halo_send.at[side],
            recv_sem=halo_recv.at[side],
            device_id={"rline": right if side == 0 else left},
            device_id_type=MESH,
        )

    def fold_copy(step, slot):
        return pltpu.make_async_remote_copy(
            src_ref=fold_own_ref,
            dst_ref=fold_all_ref.at[slot],
            send_sem=fold_send.at[step],
            recv_sem=fold_recv.at[step],
            device_id={"shot": peer(step)},
            device_id_type=MESH,
        )

    piece = share // PIECES

    def out_copy(target, p, slot):
        return pltpu.make_async_remote_copy(
            src_ref=sent_ref.at[target, p],
            dst_ref=held_ref.at[slot, p],
            send_sem=out_send.at[target, p],
            recv_sem=out_recv.at[slot, p],
            device_id={"shot": target},
            device_id_type=MESH,
        )

    pl.semaphore_wait(barrier, peers + 2)
    for side in range(2):
        halo(side).start()
    for step in range(peers):
        fold_copy(step, me).start()
    fold_all_ref[me] = fold_own_ref[...]

    def shot_blocks(items):
        blocks = [
            (window_ref.at[g], (target * share + p * piece) // 2) for target, p in items for g in range(groups)
        ]
        terms = fan_terms(blocks, shot_table_ref, piece // 2)
        for n, (target, p) in enumerate(items):
            for g in range(groups):
                begin = (target * share + p * piece + RIM) * 16 + 8
                centre = plain_ref[g, begin : begin + piece * 16].reshape(piece, 16, LANES)
                sent_ref[target, p, g] = (centre - terms[n * groups + g]).astype(BF16)
        for target, p in items:

            @pl.when(me != target)
            def _(target=target, p=p):
                out_copy(target, p, me).start()

    inner = range(1, shot_size - 1)
    for p in range(PIECES - 1):
        shot_blocks([(target, p) for target in inner])

    keeps = ((line > 0).astype(F32), (line < rline_size - 1).astype(F32))
    for side in range(2):
        halo(side).wait_recv()
        land = (RIM + receivers) * 16 + 8 if side else 8
        for g in range(groups):
            edge = halo_in_ref[side, g].astype(F32).reshape(RIM * 16, LANES)
            plain_ref[g, land : land + RIM * 16] = edge * keeps[side]
    for g in range(groups):
        for first in (0, span_pairs - step_pairs):
            fill_windows(plain_ref.at[g], window_ref.at[g], first, step_pairs)
    shot_blocks([(target, p) for p in range(PIECES) for target in (0, shot_size - 1)])
    shot_blocks([(target, PIECES - 1) for target in inner])
    held_ref[me] = sent_ref[me]

    loads[1].wait()
    build_table(rcv_taps_ref, rcv_table_ref)
    for step in range(peers):
        fold_copy(step, source(step)).wait_recv()
    folds = fold_all_ref[...].reshape(shot_size * 8, LANES).astype(F32)
    take = lax.broadcasted_iota(jnp.int32, (16, LANES), 1) == (
        me * share + lax.broadcasted_iota(jnp.int32, (16, LANES), 0)
    )
    mine = lax.dot_general(
        take.astype(F32), folds, (((1,), (1,)), ((), ())), preferred_element_type=F32
    )
    entry = lax.broadcasted_iota(jnp.int32, (shot_size * 8, rows), 0)
    shot = lax.broadcasted_iota(jnp.int32, (shot_size * 8, rows), 1) // CHUNKS
    spread = ((entry // 8) * shot_dev + entry % 8 == shot) & (entry % 8 < shot_dev)
    spread = spread.astype(F32)
    labels = jnp.dot(mine, spread, preferred_element_type=F32)
    live = jnp.sum((labels >= 0.0).astype(F32), axis=1, keepdims=True) / CHUNKS
    gains = jnp.broadcast_to(jnp.sqrt(shots / live), (16, LANES))
    chunk = (lax.broadcasted_iota(jnp.int32, (16, rows), 1) % CHUNKS).astype(F32)
    labels = jnp.where(labels >= 0.0, labels * CHUNKS + chunk, -1.0)
    columns = lax.dot_general(spread, mine, (((0,), (1,)), ((), ())), preferred_element_type=F32)
    chunk = (lax.broadcasted_iota(jnp.int32, (rows, 16), 0) % CHUNKS).astype(F32)
    columns = jnp.where(columns >= 0.0, columns * CHUNKS + chunk, -1.0)
    down = lax.broadcasted_iota(jnp.int32, (rows, rows), 0).astype(F32)
    across = lax.broadcasted_iota(jnp.int32, (rows, rows), 1).astype(F32)
    for k in range(share):
        gain_ref[k] = jnp.broadcast_to(gains[k : k + 1], (CHUNKS, LANES))
        pick_ref[k] = jnp.where(labels[k : k + 1] == down, 1.0, 0.0).astype(BF16)
        unpick_ref[k] = jnp.where(columns[:, k : k + 1] == across, 1.0, 0.0).astype(BF16)

    for slot in range(2):
        stack_ref[slot, 0 : RIM * 16 + 8] = jnp.zeros((RIM * 16 + 8, LANES), F32)
        end = (RIM + shots) * 16 + 8
        stack_ref[slot, end:] = jnp.zeros((stack_ref.shape[1] - end, LANES), F32)

    def back_copy(pair, step, owner):
        return pltpu.make_async_remote_copy(
            src_ref=back_ref.at[pair, peer(step)],
            dst_ref=out_ref.at[:, pl.ds(owner * share + 2 * pair, 2)],
            send_sem=back_send.at[pair, step],
            recv_sem=back_recv.at[pair, step],
            device_id={"shot": peer(step)},
            device_id_type=MESH,
        )

    def prepare(pair):
        slot = pair % 2
        for side in range(2):
            k = 2 * pair + side
            x = held_ref[:, k // piece, :, k % piece].reshape(rows, LANES)
            stack = jnp.dot(pick_ref[k], x, preferred_element_type=F32)
            for p in range(shots):
                begin = (RIM + p) * 16 + 8 + side * CHUNKS
                stack_ref[slot, begin : begin + CHUNKS] = stack[p * CHUNKS : (p + 1) * CHUNKS]
        for i in range(4):
            fill_windows(stack_ref.at[slot], rcv_window_ref.at[slot], i * 6, 6)

    def finish(pair):
        slot = pair % 2
        (terms,) = fan_terms([(rcv_window_ref.at[slot], 0)], rcv_table_ref, shots // 2)
        begin = RIM * 16 + 8
        value = stack_ref[slot, begin : begin + shots * 16].reshape(shots, 16, LANES) - terms
        for side in range(2):
            k = 2 * pair + side
            own = value[:, side * CHUNKS : (side + 1) * CHUNKS] * gain_ref[k][None]
            back = jnp.dot(
                unpick_ref[k], own.reshape(rows, LANES).astype(BF16), preferred_element_type=F32
            )
            back_ref[pair, :, :, side] = back.astype(BF16).reshape(shot_size, groups, 16, LANES)
        for step in range(peers):
            back_copy(pair, step, me).start()
        out_ref[:, pl.ds(me * share + 2 * pair, 2)] = back_ref[pair, me]

    def arrive(p):
        for step in range(peers):
            out_copy(peer(step), p, source(step)).wait_recv()

    pairs = share // 2
    arrive(0)
    prepare(0)
    for pair in range(pairs):
        if pair + 1 < pairs:
            if (2 * (pair + 1)) % piece == 0:
                arrive((2 * (pair + 1)) // piece)
            prepare(pair + 1)
        finish(pair)

    for side in range(2):
        halo(side).wait_send()
    for step in range(peers):
        fold_copy(step, me).wait_send()
        for p in range(PIECES):
            out_copy(peer(step), p, me).wait_send()
    for pair in range(pairs):
        for step in range(peers):
            back_copy(pair, step, me).wait_send()
            back_copy(pair, step, source(step)).wait_recv()


def shards(traces, kernels_shot, kernels_rcv, dest, gather, fold, counts):
    shot_dev, rcv_dev, samples = traces.shape
    shot_size = lax.axis_size("shot")
    rline_size = lax.axis_size("rline")
    shots = shot_dev * shot_size
    share = rcv_dev // shot_size
    rows = shots * CHUNKS
    groups = shot_dev // 2
    peers = shot_size - 1
    pairs = share // 2
    span = rcv_dev + 2 * RIM
    dma = pltpu.SemaphoreType.DMA
    vmem = pltpu.VMEM
    returned = pl.pallas_call(
        functools.partial(survey_kernel, shot_size, rline_size),
        out_shape=jax.ShapeDtypeStruct((groups, rcv_dev, 16, LANES), BF16),
        in_specs=[pl.BlockSpec(memory_space=pl.ANY)] * 5,
        out_specs=pl.BlockSpec(memory_space=vmem),
        scratch_shapes=[
            vmem(traces.shape, BF16),
            vmem(dest.shape, jnp.int32),
            vmem(fold.shape, jnp.int32),
            vmem(kernels_shot.shape, BF16),
            vmem(kernels_rcv.shape, BF16),
            vmem((8, LANES), F32),
            vmem((LANES, shot_dev * LANES), F32),
            vmem((groups, span * 16 + 16, LANES), F32),
            vmem((groups, 4, span // 2, 16, LANES), BF16),
            vmem((2, 1024, 256), BF16),
            vmem((2, 1024, 256), BF16),
            vmem((2, groups, RIM, 16, LANES), BF16),
            vmem((2, groups, RIM, 16, LANES), BF16),
            vmem((8, LANES), jnp.int32),
            vmem((shot_size, 8, LANES), jnp.int32),
            vmem((share, CHUNKS, LANES), F32),
            vmem((share, rows, rows), BF16),
            vmem((share, rows, rows), BF16),
            vmem((shot_size, PIECES, groups, share // PIECES, 16, LANES), BF16),
            vmem((shot_size, PIECES, groups, share // PIECES, 16, LANES), BF16),
            vmem((2, (shots + 16) * 16 + 16, LANES), F32),
            vmem((2, 4, shots // 2 + 8, 16, LANES), BF16),
            vmem((pairs, shot_size, groups, 2, 16, LANES), BF16),
            dma((5,)),
            dma((2,)),
            dma((2,)),
            dma((peers,)),
            dma((peers,)),
            dma((shot_size, PIECES)),
            dma((shot_size, PIECES)),
            dma((pairs, peers)),
            dma((pairs, peers)),
        ],
        compiler_params=pltpu.CompilerParams(
            vmem_limit_bytes=48 << 20, collective_id=0, has_side_effects=True
        ),
        cost_estimate=pl.CostEstimate(flops=7 * 10**9, bytes_accessed=4 * 10**6, transcendentals=0),
    )(traces, dest, fold, kernels_shot, kernels_rcv)
    result = returned.reshape(groups, rcv_dev, 2, CHUNKS, LANES).transpose(0, 2, 1, 3, 4)
    return result.reshape(shot_dev, rcv_dev, samples).astype(F32)


def solution(mesh):
    in_specs = (
        P("shot", "rline", None),
        P(),
        P(),
        P("shot", "rline"),
        P("shot", "rline"),
        P("shot", "rline"),
        P(("shot", "rline")),
    )
    out_specs = P("shot", "rline", None)
    return jax.shard_map(shards, mesh=mesh, in_specs=in_specs, out_specs=out_specs, check_vma=False)
```

time: 52.2 us -> 38.4 us (0.74)
  Pallas kernels: 46.2 us -> 32.6 us
  other arithmetic: 2.06 us -> 0.12 us
  local copies, waits for them, and re-layouts: 3.58 us -> 5.41 us
    pallas_call x1, Pallas kernels: 46.2 us -> 32.6 us  [shards(): pl.pallas_call(functools.partial(survey_kernel, shot_size, rline_size), o...]
    unnamed x5 -> x8, local copies, waits for them, and re-layouts: 1.96 us -> 3.93 us
    select_n x1 -> x0, other arithmetic: 1.25 us -> none  [shards(): cleaned = jnp.where((dest >= 0)[..., None], traces, jnp.zeros_like(traces))]
    ge x1 -> x0, other arithmetic: 0.69 us -> none  [shards(): cleaned = jnp.where((dest >= 0)[..., None], traces, jnp.zeros_like(traces))]
where the time goes in v3:
time: 38.4 us; the launch traced here: 38.2 us
  Pallas kernels  32.6 us (85%)
  local copies, waits for them, and re-layouts  5.41 us (14%)
    pallas_call x1, Pallas kernels, shards(): pl.pallas_call(functools.partial(survey_kernel, shot_size, rline_size), o...  32.6 us
    unnamed x8, local copies, waits for them, and re-layouts  3.93 us
    convert_element_type x2, local copies, waits for them, and re-layouts, shards(): return result.reshape(shot_dev, rcv_dev, samples).astype(F32)  1.48 us

profile of v3, /device:TPU:1, one launch (start us, length us, event | category | flops | bytes accessed | tf_op | source)
XLA Modules:
  0.0 38.2 jit_solution(6270645806479957367)
XLA Ops:
  0.0 0.7 %copy.6.shot_taps_hbm = bf16[4,15,31]{2,1,0:T(8,128)(2,1)S(1)} copy(bf16[4,15,31]{2,0,1:T(4,128)(2,1)} %param.8) | data formatting | bytes 7440 | tf_op args[1]
  0.7 0.7 %copy.7.rcv_taps_hbm = bf16[4,15,31]{2,1,0:T(8,128)(2,1)S(1)} copy(bf16[4,15,31]{2,0,1:T(4,128)(2,1)} %param.9) | data formatting | bytes 7440 | tf_op args[2]
  1.4 0.0 copy-start
  1.4 1.1 %copy-done = bf16[4,96,1024]{2,1,0:T(8,128)(2,1)S(1)} copy-done((bf16[4,96,1024]{2,1,0:T(8,128)(2,1)S(1)}, bf16[4,96,1024]{2,1,0:T(8,128)(2,1)}, u32[]{:S(2)}) %copy-start) | copy-done | bytes 786456
  2.6 0.0 copy-start.1
  2.6 0.7 %copy-done.1 = s32[4,96]{1,0:T(4,128)S(1)} copy-done((s32[4,96]{1,0:T(4,128)S(1)}, s32[4,96]{1,0:T(4,128)}, u32[]{:S(2)}) %copy-start.1) | copy-done | bytes 1560
  3.3 0.0 copy-start.2
  3.3 0.7 %copy-done.2 = s32[4,96]{1,0:T(4,128)S(1)} copy-done((s32[4,96]{1,0:T(4,128)S(1)}, s32[4,96]{1,0:T(4,128)}, u32[]{:S(2)}) %copy-start.2) | copy-done | bytes 1560
  3.9 32.6 %shard_map.55 = bf16[2,96,16,128]{3,2,1,0:T(8,128)(2,1)S(1)} custom-call(bf16[4,96,1024]{2,1,0:T(8,128)(2,1)S(1)} %copy-done, s32[4,96]{1,0:T(4,128)S(1)} %copy-done.1, s32[4,96]{1,0:T(4,128)S(1)} %copy-done.2, bf16[4,15,31]{2,1,0:T(8,128)(2,1)S(1)} %copy.6.shot_taps_hbm, bf16[4,15,31]{2,1,0:T(8,128)(2,1)S(1)} %copy.7.rcv_taps_hbm), custom_call_target="tpu_custom_call" | custom-call | flops 7000000000 | bytes 4000000 | tf_op jit(solution)/shard_map/pallas_call | solution.py:427
  36.5 0.1 convert_bitcast_fusion
  36.7 0.1 copy.8
  36.8 1.4 %reshape.6 = f32[4,96,1024]{2,1,0:T(8,128)} reshape(f32[2,2,96,8,128]{4,3,2,1,0:T(8,128)S(1)} %copy.8) | data formatting | bytes 3145728 | tf_op jit(solution)/shard_map/convert_element_type | solution.py:472
Async XLA Ops:
  1.4 1.1 %copy-start = (bf16[4,96,1024]{2,1,0:T(8,128)(2,1)S(1)}, bf16[4,96,1024]{2,1,0:T(8,128)(2,1)}, u32[]{:S(2)}) copy-start(bf16[4,96,1024]{2,1,0:T(8,128)(2,1)} %traces_hbm.1) | copy-start | bytes 2359300
  2.6 0.7 %copy-start.1 = (s32[4,96]{1,0:T(4,128)S(1)}, s32[4,96]{1,0:T(4,128)}, u32[]{:S(2)}) copy-start(s32[4,96]{1,0:T(4,128)} %dest_hbm.1) | copy-start | bytes 4612
  3.3 0.7 %copy-start.2 = (s32[4,96]{1,0:T(4,128)S(1)}, s32[4,96]{1,0:T(4,128)}, u32[]{:S(2)}) copy-start(s32[4,96]{1,0:T(4,128)} %fold_hbm.1) | copy-start | bytes 4612

commit v4 on v3

--- a/solution.py
+++ b/solution.py
@@ -20,22 +20,24 @@
     return lax.broadcasted_iota(jnp.int32, shape, len(shape) - 1)
 
 
-def build_table(kernel_ref, table_ref):
-    taps = kernel_ref.shape[2]
-    tap = lax.broadcasted_iota(jnp.int32, (taps, LANES), 0)
-    lane = lax.broadcasted_iota(jnp.int32, (taps, LANES), 1)
-    place_low = (lane == LANES - 1 - tap).astype(BF16)
-    place_high = (lane == LANES // 2 - 1 - tap).astype(BF16)
+def build_table(kernel_ref, rows_ref, table_ref):
+    reach, fans, taps = kernel_ref.shape
+    rows_ref[...] = jnp.zeros(rows_ref.shape, F32)
+    for step in range(reach):
+        rows_ref[step * 8 : step * 8 + fans, 0:taps] = kernel_ref[step].astype(F32)
+    tap = lax.broadcasted_iota(jnp.int32, (LANES, LANES), 0)
+    lane = lax.broadcasted_iota(jnp.int32, (LANES, LANES), 1)
+    flat = rows_ref[...].astype(BF16)
+    low = jnp.dot(flat, (lane == LANES - 1 - tap).astype(BF16), preferred_element_type=F32)
+    high = jnp.dot(flat, (lane == LANES // 2 - 1 - tap).astype(BF16), preferred_element_type=F32)
     even = (lane_index((64, LANES)) // 32) % 2 == 0
     for half in range(2):
-        base = jnp.dot(kernel_ref[2 * half], place_low, preferred_element_type=F32) + jnp.dot(
-            kernel_ref[2 * half + 1], place_high, preferred_element_type=F32
-        )
         before = jnp.zeros((64, LANES), F32)
         columns = slice(half * LANES, (half + 1) * LANES)
         for step in range(16):
-            if step < 15:
-                row = jnp.broadcast_to(base[step : step + 1], (64, LANES))
+            if step < reach:
+                at = step * 8 + 2 * half
+                row = jnp.broadcast_to(low[at : at + 1] + high[at + 1 : at + 2], (64, LANES))
                 here = pltpu.roll(row, 0, 1, stride=1, stride_axis=0)
             else:
                 here = jnp.zeros((64, LANES), F32)
@@ -135,6 +137,7 @@
     fold_ref,
     shot_taps_ref,
     rcv_taps_ref,
+    taps_rows_ref,
     alive_ref,
     mask_ref,
     plain_ref,
@@ -162,6 +165,7 @@
     out_recv,
     back_send,
     back_recv,
+    own_sem,
 ):
     shot_dev, receivers = traces_ref.shape[0], traces_ref.shape[1]
     groups = shot_dev // 2
@@ -171,7 +175,8 @@
     rows = shots * CHUNKS
     me = lax.axis_index("shot")
     line = lax.axis_index("rline")
-    right, left = lax.rem(line + 1, rline_size), lax.rem(line + rline_size - 1, rline_size)
+    has = (line > 0, line < rline_size - 1)
+    beside = (jnp.maximum(line - 1, 0), jnp.minimum(line + 1, rline_size - 1))
 
     def peer(step):
         return lax.rem(me + 1 + step, shot_size)
@@ -196,13 +201,16 @@
     barrier = pltpu.get_barrier_semaphore()
     for step in range(peers):
         pl.semaphore_signal(barrier, inc=1, device_id={"shot": peer(step)}, device_id_type=MESH)
-    for side in (left, right):
-        pl.semaphore_signal(barrier, inc=1, device_id={"rline": side}, device_id_type=MESH)
+    for side in range(2):
+
+        @pl.when(has[side])
+        def _(side=side):
+            pl.semaphore_signal(barrier, inc=1, device_id={"rline": beside[side]}, device_id_type=MESH)
 
     alive_ref[...] = jnp.zeros(alive_ref.shape, F32)
     fold_own_ref[...] = jnp.full(fold_own_ref.shape, -1, jnp.int32)
     loads[0].wait()
-    build_table(shot_taps_ref, shot_table_ref)
+    build_table(shot_taps_ref, taps_rows_ref, shot_table_ref)
     loads[2].wait()
     alive_ref[0:shot_dev, 0:receivers] = (dest_ref[...] >= 0).astype(F32)
     pick_shot = lax.broadcasted_iota(jnp.int32, (8, shot_dev * LANES), 0) == (
@@ -245,7 +253,7 @@
             dst_ref=halo_in_ref.at[side],
             send_sem=halo_send.at[side],
             recv_sem=halo_recv.at[side],
-            device_id={"rline": right if side == 0 else left},
+            device_id={"rline": beside[1 - side]},
             device_id_type=MESH,
         )
 
@@ -271,9 +279,12 @@
             device_id_type=MESH,
         )
 
-    pl.semaphore_wait(barrier, peers + 2)
+    pl.semaphore_wait(barrier, peers + has[0].astype(jnp.int32) + has[1].astype(jnp.int32))
     for side in range(2):
-        halo(side).start()
+
+        @pl.when(has[1 - side])
+        def _(side=side):
+            halo(side).start()
     for step in range(peers):
         fold_copy(step, me).start()
     fold_all_ref[me] = fold_own_ref[...]
@@ -298,13 +309,21 @@
     for p in range(PIECES - 1):
         shot_blocks([(target, p) for target in inner])
 
-    keeps = ((line > 0).astype(F32), (line < rline_size - 1).astype(F32))
     for side in range(2):
-        halo(side).wait_recv()
         land = (RIM + receivers) * 16 + 8 if side else 8
-        for g in range(groups):
-            edge = halo_in_ref[side, g].astype(F32).reshape(RIM * 16, LANES)
-            plain_ref[g, land : land + RIM * 16] = edge * keeps[side]
+
+        @pl.when(has[side])
+        def _(side=side, land=land):
+            halo(side).wait_recv()
+            for g in range(groups):
+                edge = halo_in_ref[side, g].astype(F32).reshape(RIM * 16, LANES)
+                plain_ref[g, land : land + RIM * 16] = edge
+
+        @pl.when(jnp.logical_not(has[side]))
+        def _(land=land):
+            for g in range(groups):
+                plain_ref[g, land : land + RIM * 16] = jnp.zeros((RIM * 16, LANES), F32)
+
     for g in range(groups):
         for first in (0, span_pairs - step_pairs):
             fill_windows(plain_ref.at[g], window_ref.at[g], first, step_pairs)
@@ -313,7 +332,7 @@
     held_ref[me] = sent_ref[me]
 
     loads[1].wait()
-    build_table(rcv_taps_ref, rcv_table_ref)
+    build_table(rcv_taps_ref, taps_rows_ref, rcv_table_ref)
     for step in range(peers):
         fold_copy(step, source(step)).wait_recv()
     folds = fold_all_ref[...].reshape(shot_size * 8, LANES).astype(F32)
@@ -357,6 +376,11 @@
             device_id_type=MESH,
         )
 
+    def back_own(pair):
+        return pltpu.make_async_copy(
+            back_ref.at[pair, me], out_ref.at[:, pl.ds(me * share + 2 * pair, 2)], own_sem.at[pair]
+        )
+
     def prepare(pair):
         slot = pair % 2
         for side in range(2):
@@ -383,7 +407,7 @@
             back_ref[pair, :, :, side] = back.astype(BF16).reshape(shot_size, groups, 16, LANES)
         for step in range(peers):
             back_copy(pair, step, me).start()
-        out_ref[:, pl.ds(me * share + 2 * pair, 2)] = back_ref[pair, me]
+        back_own(pair).start()
 
     def arrive(p):
         for step in range(peers):
@@ -400,12 +424,17 @@
         finish(pair)
 
     for side in range(2):
-        halo(side).wait_send()
+
+        @pl.when(has[1 - side])
+        def _(side=side):
+            halo(side).wait_send()
+
     for step in range(peers):
         fold_copy(step, me).wait_send()
         for p in range(PIECES):
             out_copy(peer(step), p, me).wait_send()
     for pair in range(pairs):
+        back_own(pair).wait()
         for step in range(peers):
             back_copy(pair, step, me).wait_send()
             back_copy(pair, step, source(step)).wait_recv()
@@ -422,19 +451,21 @@
     peers = shot_size - 1
     pairs = share // 2
     span = rcv_dev + 2 * RIM
+    fans, trace_taps, sample_taps = kernels_shot.shape
     dma = pltpu.SemaphoreType.DMA
     vmem = pltpu.VMEM
     returned = pl.pallas_call(
         functools.partial(survey_kernel, shot_size, rline_size),
         out_shape=jax.ShapeDtypeStruct((groups, rcv_dev, 16, LANES), BF16),
-        in_specs=[pl.BlockSpec(memory_space=pl.ANY)] * 5,
-        out_specs=pl.BlockSpec(memory_space=vmem),
+        in_specs=[pl.BlockSpec(memory_space=pltpu.HBM)] * 5,
+        out_specs=pl.BlockSpec(memory_space=pltpu.HBM),
         scratch_shapes=[
             vmem(traces.shape, BF16),
             vmem(dest.shape, jnp.int32),
             vmem(fold.shape, jnp.int32),
-            vmem(kernels_shot.shape, BF16),
-            vmem(kernels_rcv.shape, BF16),
+            vmem((trace_taps, fans, sample_taps), BF16),
+            vmem((trace_taps, fans, sample_taps), BF16),
+            vmem((LANES, LANES), F32),
             vmem((8, LANES), F32),
             vmem((LANES, shot_dev * LANES), F32),
             vmem((groups, span * 16 + 16, LANES), F32),
@@ -462,12 +493,13 @@
             dma((shot_size, PIECES)),
             dma((pairs, peers)),
             dma((pairs, peers)),
+            dma((pairs,)),
         ],
         compiler_params=pltpu.CompilerParams(
-            vmem_limit_bytes=48 << 20, collective_id=0, has_side_effects=True
+            vmem_limit_bytes=61 << 20, collective_id=0, has_side_effects=True
         ),
         cost_estimate=pl.CostEstimate(flops=7 * 10**9, bytes_accessed=4 * 10**6, transcendentals=0),
-    )(traces, dest, fold, kernels_shot, kernels_rcv)
+    )(traces, dest, fold, kernels_shot.transpose(1, 0, 2), kernels_rcv.transpose(1, 0, 2))
     result = returned.reshape(groups, rcv_dev, 2, CHUNKS, LANES).transpose(0, 2, 1, 3, 4)
     return result.reshape(shot_dev, rcv_dev, samples).astype(F32)
 

time: 38.4 us -> 33.4 us (0.87)
  the two profiles are of different devices: /device:TPU:1 before, /device:TPU:25 now
where the time goes in v4:
time: 33.4 us; the launch traced here: 33.2 us
  Pallas kernels  30.5 us (91%)
  local copies, waits for them, and re-layouts  1.48 us (4%)
  other arithmetic  1.25 us (4%)
    pallas_call x1, Pallas kernels, shards(): pl.pallas_call(functools.partial(survey_kernel, shot_size, rline_size), o...  30.5 us
    convert_element_type x2, local copies, waits for them, and re-layouts, shards(): return result.reshape(shot_dev, rcv_dev, samples).astype(F32)  1.48 us
    convert_element_type x1, other arithmetic, shards(): return result.reshape(shot_dev, rcv_dev, samples).astype(F32)  1.25 us

profile of v4, /device:TPU:25, one launch (start us, length us, event | category | flops | bytes accessed | tf_op | source)
XLA Modules:
  0.0 33.2 jit_solution(17123055544404058516)
XLA Ops:
  0.0 30.5 %shard_map.55 = bf16[2,96,16,128]{3,2,1,0:T(8,128)(2,1)} custom-call(bf16[4,96,1024]{2,1,0:T(8,128)(2,1)} %traces_hbm.1, s32[4,96]{1,0:T(4,128)} %dest_hbm.1, s32[4,96]{1,0:T(4,128)} %fold_hbm.1, bf16[15,4,31]{2,1,0:T(4,128)(2,1)} %bitcast.9, bf16[15,4,31]{2,1,0:T(4,128)(2,1)} %bitcast.10), custom_call_target="tpu_custom_call" | custom-call | flops 7000000000 | bytes 4000000 | tf_op jit(solution)/shard_map/pallas_call | solution.py:457
  30.5 1.2 %convert_bitcast_fusion = f32[2,2,96,8,128]{4,3,1,2,0:T(8,128)S(1)} fusion(bf16[2,96,16,128]{3,2,1,0:T(8,128)(2,1)} %shard_map.55), kind=kLoop, calls=%fused_computation | loop fusion | flops 393216 | bytes 2359296 | tf_op jit(solution)/shard_map/convert_element_type | solution.py:504
  31.7 0.1 copy.6
  31.8 1.4 %reshape.6 = f32[4,96,1024]{2,1,0:T(8,128)} reshape(f32[2,2,96,8,128]{4,3,2,1,0:T(8,128)S(1)} %copy.6) | data formatting | bytes 3145728 | tf_op jit(solution)/shard_map/convert_element_type | solution.py:504

commit v5 on v4

--- a/solution.py
+++ b/solution.py
@@ -149,7 +149,6 @@
     fold_own_ref,
     fold_all_ref,
     gain_ref,
-    pick_ref,
     unpick_ref,
     sent_ref,
     held_ref,
@@ -192,8 +191,8 @@
                 (rcv_taps_hbm, rcv_taps_ref),
                 (dest_hbm, dest_ref),
                 (fold_hbm, fold_ref),
-                (traces_hbm, traces_ref),
             ]
+            + [(traces_hbm.at[s], traces_ref.at[s]) for s in range(shot_dev)]
         )
     ]
     for load in loads:
@@ -211,6 +210,8 @@
     fold_own_ref[...] = jnp.full(fold_own_ref.shape, -1, jnp.int32)
     loads[0].wait()
     build_table(shot_taps_ref, taps_rows_ref, shot_table_ref)
+    loads[1].wait()
+    build_table(rcv_taps_ref, taps_rows_ref, rcv_table_ref)
     loads[2].wait()
     alive_ref[0:shot_dev, 0:receivers] = (dest_ref[...] >= 0).astype(F32)
     pick_shot = lax.broadcasted_iota(jnp.int32, (8, shot_dev * LANES), 0) == (
@@ -219,14 +220,12 @@
     mask_ref[...] = lax.dot_general(
         alive_ref[...], pick_shot.astype(F32), (((0,), (0,)), ((), ())), preferred_element_type=F32
     )
-    loads[4].wait()
     for s in range(shot_dev):
-
-        @pl.loop(0, receivers // 16)
-        def _(i):
+        loads[4 + s].wait()
+        for i in range(receivers // 16):
             x = traces_ref[s, pl.ds(i * 16, 16)].astype(F32)
             for half in range(2):
-                mask = mask_ref[pl.ds(i * 16 + half * 8, 8), s * LANES : (s + 1) * LANES]
+                mask = mask_ref[i * 16 + half * 8 : i * 16 + half * 8 + 8, s * LANES : (s + 1) * LANES]
                 begin = (i * 16 + half * 8 + RIM) * 16 + 8 + (s % 2) * CHUNKS
                 for c in range(CHUNKS):
                     piece = x[half * 8 : half * 8 + 8, c * LANES : (c + 1) * LANES]
@@ -243,8 +242,7 @@
     span_pairs = (receivers + 2 * RIM) // 2
     for g in range(groups):
 
-        @pl.loop(1, span_pairs // step_pairs - 1)
-        def _(i):
+        for i in range(1, span_pairs // step_pairs - 1):
             fill_windows(plain_ref.at[g], window_ref.at[g], i * step_pairs, step_pairs)
 
     def halo(side):
@@ -331,8 +329,6 @@
     shot_blocks([(target, PIECES - 1) for target in inner])
     held_ref[me] = sent_ref[me]
 
-    loads[1].wait()
-    build_table(rcv_taps_ref, taps_rows_ref, rcv_table_ref)
     for step in range(peers):
         fold_copy(step, source(step)).wait_recv()
     folds = fold_all_ref[...].reshape(shot_size * 8, LANES).astype(F32)
@@ -358,8 +354,6 @@
     across = lax.broadcasted_iota(jnp.int32, (rows, rows), 1).astype(F32)
     for k in range(share):
         gain_ref[k] = jnp.broadcast_to(gains[k : k + 1], (CHUNKS, LANES))
-        pick_ref[k] = jnp.where(labels[k : k + 1] == down, 1.0, 0.0).astype(BF16)
-        unpick_ref[k] = jnp.where(columns[:, k : k + 1] == across, 1.0, 0.0).astype(BF16)
 
     for slot in range(2):
         stack_ref[slot, 0 : RIM * 16 + 8] = jnp.zeros((RIM * 16 + 8, LANES), F32)
@@ -386,7 +380,9 @@
         for side in range(2):
             k = 2 * pair + side
             x = held_ref[:, k // piece, :, k % piece].reshape(rows, LANES)
-            stack = jnp.dot(pick_ref[k], x, preferred_element_type=F32)
+            pick = jnp.where(labels[k : k + 1] == down, 1.0, 0.0).astype(BF16)
+            unpick_ref[k] = jnp.where(columns[:, k : k + 1] == across, 1.0, 0.0).astype(BF16)
+            stack = jnp.dot(pick, x, preferred_element_type=F32)
             for p in range(shots):
                 begin = (RIM + p) * 16 + 8 + side * CHUNKS
                 stack_ref[slot, begin : begin + CHUNKS] = stack[p * CHUNKS : (p + 1) * CHUNKS]
@@ -478,13 +474,12 @@
             vmem((shot_size, 8, LANES), jnp.int32),
             vmem((share, CHUNKS, LANES), F32),
             vmem((share, rows, rows), BF16),
-            vmem((share, rows, rows), BF16),
             vmem((shot_size, PIECES, groups, share // PIECES, 16, LANES), BF16),
             vmem((shot_size, PIECES, groups, share // PIECES, 16, LANES), BF16),
             vmem((2, (shots + 16) * 16 + 16, LANES), F32),
             vmem((2, 4, shots // 2 + 8, 16, LANES), BF16),
             vmem((pairs, shot_size, groups, 2, 16, LANES), BF16),
-            dma((5,)),
+            dma((4 + shot_dev,)),
             dma((2,)),
             dma((2,)),
             dma((peers,)),

time: 33.4 us -> 32.6 us (0.976)
  Pallas kernels: 30.5 us -> 29.7 us
    pallas_call x1, Pallas kernels: 30.5 us -> 29.7 us  [shards(): pl.pallas_call(functools.partial(survey_kernel, shot_size, rline_size), o...]
where the time goes in v5:
time: 32.6 us; the launch traced here: 32.5 us
  Pallas kernels  29.7 us (91%)
  local copies, waits for them, and re-layouts  1.48 us (5%)
  other arithmetic  1.25 us (4%)
    pallas_call x1, Pallas kernels, shards(): pl.pallas_call(functools.partial(survey_kernel, shot_size, rline_size), o...  29.7 us
    convert_element_type x2, local copies, waits for them, and re-layouts, shards(): return result.reshape(shot_dev, rcv_dev, samples).astype(F32)  1.48 us
    convert_element_type x1, other arithmetic, shards(): return result.reshape(shot_dev, rcv_dev, samples).astype(F32)  1.25 us

profile of v5, /device:TPU:25, one launch (start us, length us, event | category | flops | bytes accessed | tf_op | source)
XLA Modules:
  0.0 32.5 jit_solution(3629891700883245340)
XLA Ops:
  0.0 29.7 %shard_map.55 = bf16[2,96,16,128]{3,2,1,0:T(8,128)(2,1)} custom-call(bf16[4,96,1024]{2,1,0:T(8,128)(2,1)} %traces_hbm.1, s32[4,96]{1,0:T(4,128)} %dest_hbm.1, s32[4,96]{1,0:T(4,128)} %fold_hbm.1, bf16[15,4,31]{2,1,0:T(4,128)(2,1)} %bitcast.9, bf16[15,4,31]{2,1,0:T(4,128)(2,1)} %bitcast.10), custom_call_target="tpu_custom_call" | custom-call | flops 7000000000 | bytes 4000000 | tf_op jit(solution)/shard_map/pallas_call | solution.py:453
  29.7 1.2 %convert_bitcast_fusion = f32[2,2,96,8,128]{4,3,1,2,0:T(8,128)S(1)} fusion(bf16[2,96,16,128]{3,2,1,0:T(8,128)(2,1)} %shard_map.55), kind=kLoop, calls=%fused_computation | loop fusion | flops 393216 | bytes 2359296 | tf_op jit(solution)/shard_map/convert_element_type | solution.py:499
  31.0 0.1 copy.6
  31.1 1.4 %reshape.6 = f32[4,96,1024]{2,1,0:T(8,128)} reshape(f32[2,2,96,8,128]{4,3,2,1,0:T(8,128)S(1)} %copy.6) | data formatting | bytes 3145728 | tf_op jit(solution)/shard_map/convert_element_type | solution.py:499

commit v6 on v5

--- a/solution.py
+++ b/solution.py
@@ -12,7 +12,6 @@
 BF16 = jnp.bfloat16
 F32 = jnp.float32
 RIM = 7
-PIECES = 3
 MESH = pl.DeviceIdType.MESH
 
 
@@ -172,6 +171,9 @@
     peers = shot_size - 1
     shots = shot_size * shot_dev
     rows = shots * CHUNKS
+    order = list(range(1, share - 1)) + [0, share - 1]
+    cuts = [0, 4, 8, share - 2, share]
+    portions = list(zip(cuts, cuts[1:]))
     me = lax.axis_index("shot")
     line = lax.axis_index("rline")
     has = (line > 0, line < rline_size - 1)
@@ -238,12 +240,12 @@
     loads[3].wait()
     fold_own_ref[0:shot_dev, 0:receivers] = fold_ref[...]
 
-    step_pairs = 5
     span_pairs = (receivers + 2 * RIM) // 2
+    edge_pairs = shot_size // 2
+    inner = list(range(edge_pairs, span_pairs - edge_pairs, 5)) + [span_pairs - edge_pairs]
     for g in range(groups):
-
-        for i in range(1, span_pairs // step_pairs - 1):
-            fill_windows(plain_ref.at[g], window_ref.at[g], i * step_pairs, step_pairs)
+        for first, end in zip(inner, inner[1:]):
+            fill_windows(plain_ref.at[g], window_ref.at[g], first, end - first)
 
     def halo(side):
         return pltpu.make_async_remote_copy(
@@ -265,14 +267,13 @@
             device_id_type=MESH,
         )
 
-    piece = share // PIECES
-
-    def out_copy(target, p, slot):
+    def out_copy(target, n, slot):
+        part = pl.ds(portions[n][0], portions[n][1] - portions[n][0])
         return pltpu.make_async_remote_copy(
-            src_ref=sent_ref.at[target, p],
-            dst_ref=held_ref.at[slot, p],
-            send_sem=out_send.at[target, p],
-            recv_sem=out_recv.at[slot, p],
+            src_ref=sent_ref.at[target, part],
+            dst_ref=held_ref.at[slot, part],
+            send_sem=out_send.at[target, n],
+            recv_sem=out_recv.at[slot, n],
             device_id={"shot": target},
             device_id_type=MESH,
         )
@@ -287,25 +288,22 @@
         fold_copy(step, me).start()
     fold_all_ref[me] = fold_own_ref[...]
 
-    def shot_blocks(items):
-        blocks = [
-            (window_ref.at[g], (target * share + p * piece) // 2) for target, p in items for g in range(groups)
-        ]
-        terms = fan_terms(blocks, shot_table_ref, piece // 2)
-        for n, (target, p) in enumerate(items):
+    def shot_blocks(starts, pairs, n):
+        blocks = [(window_ref.at[g], first) for first in starts for g in range(groups)]
+        terms = fan_terms(blocks, shot_table_ref, pairs)
+        for i, first in enumerate(starts):
             for g in range(groups):
-                begin = (target * share + p * piece + RIM) * 16 + 8
-                centre = plain_ref[g, begin : begin + piece * 16].reshape(piece, 16, LANES)
-                sent_ref[target, p, g] = (centre - terms[n * groups + g]).astype(BF16)
-        for target, p in items:
-
-            @pl.when(me != target)
-            def _(target=target, p=p):
-                out_copy(target, p, me).start()
-
-    inner = range(1, shot_size - 1)
-    for p in range(PIECES - 1):
-        shot_blocks([(target, p) for target in inner])
+                begin = (2 * first + RIM) * 16 + 8
+                centre = plain_ref[g, begin : begin + pairs * 32].reshape(2 * pairs, 16, LANES)
+                value = (centre - terms[i * groups + g]).astype(BF16)
+                for m in range(2 * pairs):
+                    row, target = divmod(2 * first + m, shot_size)
+                    sent_ref[target, order.index(row), g] = value[m]
+        for step in range(peers):
+            out_copy(peer(step), n, me).start()
+
+    for n, (begin, end) in enumerate(portions[:-1]):
+        shot_blocks([order[begin] * shot_size // 2], (end - begin) * shot_size // 2, n)
 
     for side in range(2):
         land = (RIM + receivers) * 16 + 8 if side else 8
@@ -323,18 +321,17 @@
                 plain_ref[g, land : land + RIM * 16] = jnp.zeros((RIM * 16, LANES), F32)
 
     for g in range(groups):
-        for first in (0, span_pairs - step_pairs):
-            fill_windows(plain_ref.at[g], window_ref.at[g], first, step_pairs)
-    shot_blocks([(target, p) for p in range(PIECES) for target in (0, shot_size - 1)])
-    shot_blocks([(target, PIECES - 1) for target in inner])
+        for first in (0, span_pairs - edge_pairs):
+            fill_windows(plain_ref.at[g], window_ref.at[g], first, edge_pairs)
+    shot_blocks([0, (receivers - shot_size) // 2], shot_size // 2, len(portions) - 1)
     held_ref[me] = sent_ref[me]
 
     for step in range(peers):
         fold_copy(step, source(step)).wait_recv()
     folds = fold_all_ref[...].reshape(shot_size * 8, LANES).astype(F32)
-    take = lax.broadcasted_iota(jnp.int32, (16, LANES), 1) == (
-        me * share + lax.broadcasted_iota(jnp.int32, (16, LANES), 0)
-    )
+    place = lax.broadcasted_iota(jnp.int32, (16, LANES), 0)
+    place = jnp.where(place < share - 2, place + 1, jnp.where(place == share - 2, 0, place))
+    take = lax.broadcasted_iota(jnp.int32, (16, LANES), 1) == place * shot_size + me
     mine = lax.dot_general(
         take.astype(F32), folds, (((1,), (1,)), ((), ())), preferred_element_type=F32
     )
@@ -360,26 +357,36 @@
         end = (RIM + shots) * 16 + 8
         stack_ref[slot, end:] = jnp.zeros((stack_ref.shape[1] - end, LANES), F32)
 
-    def back_copy(pair, step, owner):
-        return pltpu.make_async_remote_copy(
-            src_ref=back_ref.at[pair, peer(step)],
-            dst_ref=out_ref.at[:, pl.ds(owner * share + 2 * pair, 2)],
-            send_sem=back_send.at[pair, step],
-            recv_sem=back_recv.at[pair, step],
-            device_id={"shot": peer(step)},
-            device_id_type=MESH,
-        )
+    def parts(pair):
+        one, two = order[2 * pair], order[2 * pair + 1]
+        return [(0, one, 2)] if two == one + 1 else [(0, one, 1), (1, two, 1)]
+
+    def back_copies(pair, step, owner):
+        return [
+            pltpu.make_async_remote_copy(
+                src_ref=back_ref.at[pair, peer(step), pl.ds(at, count)],
+                dst_ref=out_ref.at[pl.ds(row, count), owner],
+                send_sem=back_send.at[pair + at, step],
+                recv_sem=back_recv.at[pair + at, step],
+                device_id={"shot": peer(step)},
+                device_id_type=MESH,
+            )
+            for at, row, count in parts(pair)
+        ]
 
     def back_own(pair):
-        return pltpu.make_async_copy(
-            back_ref.at[pair, me], out_ref.at[:, pl.ds(me * share + 2 * pair, 2)], own_sem.at[pair]
-        )
+        return [
+            pltpu.make_async_copy(
+                back_ref.at[pair, me, pl.ds(at, count)], out_ref.at[pl.ds(row, count), me], own_sem.at[pair + at]
+            )
+            for at, row, count in parts(pair)
+        ]
 
     def prepare(pair):
         slot = pair % 2
         for side in range(2):
             k = 2 * pair + side
-            x = held_ref[:, k // piece, :, k % piece].reshape(rows, LANES)
+            x = held_ref[:, k].reshape(rows, LANES)
             pick = jnp.where(labels[k : k + 1] == down, 1.0, 0.0).astype(BF16)
             unpick_ref[k] = jnp.where(columns[:, k : k + 1] == across, 1.0, 0.0).astype(BF16)
             stack = jnp.dot(pick, x, preferred_element_type=F32)
@@ -400,22 +407,25 @@
             back = jnp.dot(
                 unpick_ref[k], own.reshape(rows, LANES).astype(BF16), preferred_element_type=F32
             )
-            back_ref[pair, :, :, side] = back.astype(BF16).reshape(shot_size, groups, 16, LANES)
+            back_ref[pair, :, side] = back.astype(BF16).reshape(shot_size, groups, 16, LANES)
         for step in range(peers):
-            back_copy(pair, step, me).start()
-        back_own(pair).start()
-
-    def arrive(p):
+            for copy in back_copies(pair, step, me):
+                copy.start()
+        for copy in back_own(pair):
+            copy.start()
+
+    def arrive(n):
         for step in range(peers):
-            out_copy(peer(step), p, source(step)).wait_recv()
+            out_copy(peer(step), n, source(step)).wait_recv()
 
     pairs = share // 2
     arrive(0)
     prepare(0)
     for pair in range(pairs):
         if pair + 1 < pairs:
-            if (2 * (pair + 1)) % piece == 0:
-                arrive((2 * (pair + 1)) // piece)
+            for n, (begin, _) in enumerate(portions):
+                if begin == 2 * (pair + 1):
+                    arrive(n)
             prepare(pair + 1)
         finish(pair)
 
@@ -427,13 +437,16 @@
 
     for step in range(peers):
         fold_copy(step, me).wait_send()
-        for p in range(PIECES):
-            out_copy(peer(step), p, me).wait_send()
+        for n in range(len(portions)):
+            out_copy(peer(step), n, me).wait_send()
     for pair in range(pairs):
-        back_own(pair).wait()
+        for copy in back_own(pair):
+            copy.wait()
         for step in range(peers):
-            back_copy(pair, step, me).wait_send()
-            back_copy(pair, step, source(step)).wait_recv()
+            for copy in back_copies(pair, step, me):
+                copy.wait_send()
+            for copy in back_copies(pair, step, source(step)):
+                copy.wait_recv()
 
 
 def shards(traces, kernels_shot, kernels_rcv, dest, gather, fold, counts):
@@ -452,7 +465,7 @@
     vmem = pltpu.VMEM
     returned = pl.pallas_call(
         functools.partial(survey_kernel, shot_size, rline_size),
-        out_shape=jax.ShapeDtypeStruct((groups, rcv_dev, 16, LANES), BF16),
+        out_shape=jax.ShapeDtypeStruct((share, shot_size, groups, 16, LANES), BF16),
         in_specs=[pl.BlockSpec(memory_space=pltpu.HBM)] * 5,
         out_specs=pl.BlockSpec(memory_space=pltpu.HBM),
         scratch_shapes=[
@@ -474,28 +487,28 @@
             vmem((shot_size, 8, LANES), jnp.int32),
             vmem((share, CHUNKS, LANES), F32),
             vmem((share, rows, rows), BF16),
-            vmem((shot_size, PIECES, groups, share // PIECES, 16, LANES), BF16),
-            vmem((shot_size, PIECES, groups, share // PIECES, 16, LANES), BF16),
+            vmem((shot_size, share, groups, 16, LANES), BF16),
+            vmem((shot_size, share, groups, 16, LANES), BF16),
             vmem((2, (shots + 16) * 16 + 16, LANES), F32),
             vmem((2, 4, shots // 2 + 8, 16, LANES), BF16),
-            vmem((pairs, shot_size, groups, 2, 16, LANES), BF16),
+            vmem((pairs, shot_size, 2, groups, 16, LANES), BF16),
             dma((4 + shot_dev,)),
             dma((2,)),
             dma((2,)),
             dma((peers,)),
             dma((peers,)),
-            dma((shot_size, PIECES)),
-            dma((shot_size, PIECES)),
-            dma((pairs, peers)),
-            dma((pairs, peers)),
-            dma((pairs,)),
+            dma((shot_size, 4)),
+            dma((shot_size, 4)),
+            dma((pairs + 1, peers)),
+            dma((pairs + 1, peers)),
+            dma((pairs + 1,)),
         ],
         compiler_params=pltpu.CompilerParams(
             vmem_limit_bytes=61 << 20, collective_id=0, has_side_effects=True
         ),
         cost_estimate=pl.CostEstimate(flops=7 * 10**9, bytes_accessed=4 * 10**6, transcendentals=0),
     )(traces, dest, fold, kernels_shot.transpose(1, 0, 2), kernels_rcv.transpose(1, 0, 2))
-    result = returned.reshape(groups, rcv_dev, 2, CHUNKS, LANES).transpose(0, 2, 1, 3, 4)
+    result = returned.reshape(rcv_dev, shot_dev, CHUNKS, LANES).transpose(1, 0, 2, 3)
     return result.reshape(shot_dev, rcv_dev, samples).astype(F32)
 
 

time: 32.6 us -> 33.6 us (1.031)
  the two profiles are of different devices: /device:TPU:25 before, /device:TPU:1 now
where the time goes in v6:
time: 33.6 us; the launch traced here: 33.5 us
  Pallas kernels  29.5 us (88%)
  local copies, waits for them, and re-layouts  2.6 us (8%)
  other arithmetic  1.34 us (4%)
    pallas_call x1, Pallas kernels, shards(): pl.pallas_call(functools.partial(survey_kernel, shot_size, rline_size), o...  29.5 us
    convert_element_type x2, local copies, waits for them, and re-layouts, shards(): return result.reshape(shot_dev, rcv_dev, samples).astype(F32)  2.6 us
    convert_element_type x1, other arithmetic, shards(): return result.reshape(shot_dev, rcv_dev, samples).astype(F32)  1.34 us

profile of v6, /device:TPU:1, one launch (start us, length us, event | category | flops | bytes accessed | tf_op | source)
XLA Modules:
  0.0 33.5 jit_solution(5095254786558714784)
XLA Ops:
  0.0 29.5 %shard_map.55 = bf16[12,8,2,16,128]{4,3,2,1,0:T(8,128)(2,1)} custom-call(bf16[4,96,1024]{2,1,0:T(8,128)(2,1)} %traces_hbm.1, s32[4,96]{1,0:T(4,128)} %dest_hbm.1, s32[4,96]{1,0:T(4,128)} %fold_hbm.1, bf16[15,4,31]{2,1,0:T(4,128)(2,1)} %bitcast.11, bf16[15,4,31]{2,1,0:T(4,128)(2,1)} %bitcast.12), custom_call_target="tpu_custom_call" | custom-call | flops 7000000000 | bytes 4000000 | tf_op jit(solution)/shard_map/pallas_call | solution.py:466
  29.5 1.3 %convert_bitcast_fusion = f32[4,96,8,128]{3,2,0,1:T(8,128)S(1)} fusion(bf16[96,4,8,128]{3,2,1,0:T(8,128)(2,1)} %bitcast.10), kind=kLoop, calls=%fused_computation | loop fusion | flops 393216 | bytes 2359296 | tf_op jit(solution)/shard_map/convert_element_type | solution.py:512
  30.9 0.5 %reshape.8 = f32[4,96,1024]{2,0,1:T(4,128)S(1)} reshape(f32[4,96,8,128]{3,2,0,1:T(8,128)S(1)} %convert_bitcast_fusion) | data formatting | bytes 3145728 | tf_op jit(solution)/shard_map/convert_element_type | solution.py:512
  31.4 2.1 %copy.7 = f32[4,96,1024]{2,1,0:T(8,128)} copy(f32[4,96,1024]{2,0,1:T(4,128)S(1)} %reshape.8) | data formatting | bytes 3145728 | tf_op jit(solution)/shard_map/convert_element_type | solution.py:512

commit v7 on v6

--- a/solution.py
+++ b/solution.py
@@ -278,17 +278,7 @@
             device_id_type=MESH,
         )
 
-    pl.semaphore_wait(barrier, peers + has[0].astype(jnp.int32) + has[1].astype(jnp.int32))
-    for side in range(2):
-
-        @pl.when(has[1 - side])
-        def _(side=side):
-            halo(side).start()
-    for step in range(peers):
-        fold_copy(step, me).start()
-    fold_all_ref[me] = fold_own_ref[...]
-
-    def shot_blocks(starts, pairs, n):
+    def shot_blocks(starts, pairs):
         blocks = [(window_ref.at[g], first) for first in starts for g in range(groups)]
         terms = fan_terms(blocks, shot_table_ref, pairs)
         for i, first in enumerate(starts):
@@ -299,11 +289,30 @@
                 for m in range(2 * pairs):
                     row, target = divmod(2 * first + m, shot_size)
                     sent_ref[target, order.index(row), g] = value[m]
+
+    def send_out(n):
         for step in range(peers):
             out_copy(peer(step), n, me).start()
 
-    for n, (begin, end) in enumerate(portions[:-1]):
-        shot_blocks([order[begin] * shot_size // 2], (end - begin) * shot_size // 2, n)
+    def inner_blocks(n):
+        begin, end = portions[n]
+        shot_blocks([order[begin] * shot_size // 2], (end - begin) * shot_size // 2)
+
+    inner_blocks(0)
+    pl.semaphore_wait(barrier, peers + has[0].astype(jnp.int32) + has[1].astype(jnp.int32))
+    for side in range(2):
+
+        @pl.when(has[1 - side])
+        def _(side=side):
+            halo(side).start()
+    for step in range(peers):
+        fold_copy(step, me).start()
+    fold_all_ref[me] = fold_own_ref[...]
+
+    for n in range(len(portions) - 1):
+        if n > 0:
+            inner_blocks(n)
+        send_out(n)
 
     for side in range(2):
         land = (RIM + receivers) * 16 + 8 if side else 8
@@ -323,7 +332,8 @@
     for g in range(groups):
         for first in (0, span_pairs - edge_pairs):
             fill_windows(plain_ref.at[g], window_ref.at[g], first, edge_pairs)
-    shot_blocks([0, (receivers - shot_size) // 2], shot_size // 2, len(portions) - 1)
+    shot_blocks([0, (receivers - shot_size) // 2], shot_size // 2)
+    send_out(len(portions) - 1)
     held_ref[me] = sent_ref[me]
 
     for step in range(peers):
@@ -364,8 +374,8 @@
     def back_copies(pair, step, owner):
         return [
             pltpu.make_async_remote_copy(
-                src_ref=back_ref.at[pair, peer(step), pl.ds(at, count)],
-                dst_ref=out_ref.at[pl.ds(row, count), owner],
+                src_ref=back_ref.at[pair, peer(step), :, pl.ds(at, count)],
+                dst_ref=out_ref.at[:, pl.ds(row, count), owner],
                 send_sem=back_send.at[pair + at, step],
                 recv_sem=back_recv.at[pair + at, step],
                 device_id={"shot": peer(step)},
@@ -377,7 +387,9 @@
     def back_own(pair):
         return [
             pltpu.make_async_copy(
-                back_ref.at[pair, me, pl.ds(at, count)], out_ref.at[pl.ds(row, count), me], own_sem.at[pair + at]
+                back_ref.at[pair, me, :, pl.ds(at, count)],
+                out_ref.at[:, pl.ds(row, count), me],
+                own_sem.at[pair + at],
             )
             for at, row, count in parts(pair)
         ]
@@ -407,7 +419,7 @@
             back = jnp.dot(
                 unpick_ref[k], own.reshape(rows, LANES).astype(BF16), preferred_element_type=F32
             )
-            back_ref[pair, :, side] = back.astype(BF16).reshape(shot_size, groups, 16, LANES)
+            back_ref[pair, :, :, side] = back.astype(BF16).reshape(shot_size, groups, 16, LANES)
         for step in range(peers):
             for copy in back_copies(pair, step, me):
                 copy.start()
@@ -465,7 +477,7 @@
     vmem = pltpu.VMEM
     returned = pl.pallas_call(
         functools.partial(survey_kernel, shot_size, rline_size),
-        out_shape=jax.ShapeDtypeStruct((share, shot_size, groups, 16, LANES), BF16),
+        out_shape=jax.ShapeDtypeStruct((groups, share, shot_size, 16, LANES), BF16),
         in_specs=[pl.BlockSpec(memory_space=pltpu.HBM)] * 5,
         out_specs=pl.BlockSpec(memory_space=pltpu.HBM),
         scratch_shapes=[
@@ -491,7 +503,7 @@
             vmem((shot_size, share, groups, 16, LANES), BF16),
             vmem((2, (shots + 16) * 16 + 16, LANES), F32),
             vmem((2, 4, shots // 2 + 8, 16, LANES), BF16),
-            vmem((pairs, shot_size, 2, groups, 16, LANES), BF16),
+            vmem((pairs, shot_size, groups, 2, 16, LANES), BF16),
             dma((4 + shot_dev,)),
             dma((2,)),
             dma((2,)),
@@ -508,7 +520,7 @@
         ),
         cost_estimate=pl.CostEstimate(flops=7 * 10**9, bytes_accessed=4 * 10**6, transcendentals=0),
     )(traces, dest, fold, kernels_shot.transpose(1, 0, 2), kernels_rcv.transpose(1, 0, 2))
-    result = returned.reshape(rcv_dev, shot_dev, CHUNKS, LANES).transpose(1, 0, 2, 3)
+    result = returned.reshape(groups, rcv_dev, 2, CHUNKS, LANES).transpose(0, 2, 1, 3, 4)
     return result.reshape(shot_dev, rcv_dev, samples).astype(F32)
 
 

time: 33.6 us -> 32.3 us (0.961)
  local copies, waits for them, and re-layouts: 2.6 us -> 1.48 us
    convert_element_type x2, local copies, waits for them, and re-layouts: 2.6 us -> 1.48 us  [shards(): return result.reshape(shot_dev, rcv_dev, samples).astype(F32)]
where the time goes in v7:
time: 32.3 us; the launch traced here: 32.1 us
  Pallas kernels  29.4 us (91%)
  local copies, waits for them, and re-layouts  1.48 us (5%)
  other arithmetic  1.25 us (4%)
    pallas_call x1, Pallas kernels, shards(): pl.pallas_call(functools.partial(survey_kernel, shot_size, rline_size), o...  29.4 us
    convert_element_type x2, local copies, waits for them, and re-layouts, shards(): return result.reshape(shot_dev, rcv_dev, samples).astype(F32)  1.48 us
    convert_element_type x1, other arithmetic, shards(): return result.reshape(shot_dev, rcv_dev, samples).astype(F32)  1.25 us

profile of v7, /device:TPU:1, one launch (start us, length us, event | category | flops | bytes accessed | tf_op | source)
XLA Modules:
  0.0 32.1 jit_solution(11686299039626656114)
XLA Ops:
  0.0 29.4 %shard_map.55 = bf16[2,12,8,16,128]{4,3,2,1,0:T(8,128)(2,1)} custom-call(bf16[4,96,1024]{2,1,0:T(8,128)(2,1)} %traces_hbm.1, s32[4,96]{1,0:T(4,128)} %dest_hbm.1, s32[4,96]{1,0:T(4,128)} %fold_hbm.1, bf16[15,4,31]{2,1,0:T(4,128)(2,1)} %bitcast.9, bf16[15,4,31]{2,1,0:T(4,128)(2,1)} %bitcast.10), custom_call_target="tpu_custom_call" | custom-call | flops 7000000000 | bytes 4000000 | tf_op jit(solution)/shard_map/pallas_call | solution.py:478
  29.4 1.2 %convert_bitcast_fusion = f32[2,2,96,8,128]{4,3,1,2,0:T(8,128)S(1)} fusion(bf16[2,96,2,8,128]{4,3,2,1,0:T(8,128)(2,1)} %bitcast.8), kind=kLoop, calls=%fused_computation | loop fusion | flops 393216 | bytes 2359296 | tf_op jit(solution)/shard_map/convert_element_type | solution.py:524
  30.6 0.1 copy.6
  30.7 1.4 %reshape.6 = f32[4,96,1024]{2,1,0:T(8,128)} reshape(f32[2,2,96,8,128]{4,3,2,1,0:T(8,128)S(1)} %copy.6) | data formatting | bytes 3145728 | tf_op jit(solution)/shard_map/convert_element_type | solution.py:524

commit v8 on v7

--- a/solution.py
+++ b/solution.py
@@ -172,18 +172,20 @@
     shots = shot_size * shot_dev
     rows = shots * CHUNKS
     order = list(range(1, share - 1)) + [0, share - 1]
-    cuts = [0, 4, 8, share - 2, share]
+    cuts = [0, 2, 6, share - 2, share]
     portions = list(zip(cuts, cuts[1:]))
     me = lax.axis_index("shot")
     line = lax.axis_index("rline")
     has = (line > 0, line < rline_size - 1)
     beside = (jnp.maximum(line - 1, 0), jnp.minimum(line + 1, rline_size - 1))
 
+    far = sorted(range(1, shot_size), key=lambda d: abs(d - shot_size // 2))
+
     def peer(step):
-        return lax.rem(me + 1 + step, shot_size)
+        return lax.rem(me + far[step], shot_size)
 
     def source(step):
-        return lax.rem(me + shot_size - 1 - step, shot_size)
+        return lax.rem(me + shot_size - far[step], shot_size)
 
     loads = [
         pltpu.make_async_copy(a, b, load_sem.at[i])
@@ -212,8 +214,6 @@
     fold_own_ref[...] = jnp.full(fold_own_ref.shape, -1, jnp.int32)
     loads[0].wait()
     build_table(shot_taps_ref, taps_rows_ref, shot_table_ref)
-    loads[1].wait()
-    build_table(rcv_taps_ref, taps_rows_ref, rcv_table_ref)
     loads[2].wait()
     alive_ref[0:shot_dev, 0:receivers] = (dest_ref[...] >= 0).astype(F32)
     pick_shot = lax.broadcasted_iota(jnp.int32, (8, shot_dev * LANES), 0) == (
@@ -242,10 +242,14 @@
 
     span_pairs = (receivers + 2 * RIM) // 2
     edge_pairs = shot_size // 2
-    inner = list(range(edge_pairs, span_pairs - edge_pairs, 5)) + [span_pairs - edge_pairs]
-    for g in range(groups):
-        for first, end in zip(inner, inner[1:]):
-            fill_windows(plain_ref.at[g], window_ref.at[g], first, end - first)
+    made = [edge_pairs]
+
+    def make_tiles(limit):
+        while made[0] < limit:
+            count = min(5, limit - made[0])
+            for g in range(groups):
+                fill_windows(plain_ref.at[g], window_ref.at[g], made[0], count)
+            made[0] += count
 
     def halo(side):
         return pltpu.make_async_remote_copy(
@@ -296,6 +300,7 @@
 
     def inner_blocks(n):
         begin, end = portions[n]
+        make_tiles((order[end - 1] + 1) * shot_size // 2 + RIM)
         shot_blocks([order[begin] * shot_size // 2], (end - begin) * shot_size // 2)
 
     inner_blocks(0)
@@ -314,6 +319,8 @@
             inner_blocks(n)
         send_out(n)
 
+    loads[1].wait()
+    build_table(rcv_taps_ref, taps_rows_ref, rcv_table_ref)
     for side in range(2):
         land = (RIM + receivers) * 16 + 8 if side else 8
 

time: 32.3 us -> 30.8 us (0.954)
  Pallas kernels: 29.4 us -> 27.9 us
    pallas_call x1, Pallas kernels: 29.4 us -> 27.9 us  [shards(): pl.pallas_call(functools.partial(survey_kernel, shot_size, rline_size), o...]
where the time goes in v8:
time: 30.8 us; the launch traced here: 30.7 us
  Pallas kernels  27.9 us (91%)
  local copies, waits for them, and re-layouts  1.48 us (5%)
  other arithmetic  1.25 us (4%)
    pallas_call x1, Pallas kernels, shards(): pl.pallas_call(functools.partial(survey_kernel, shot_size, rline_size), o...  27.9 us
    convert_element_type x2, local copies, waits for them, and re-layouts, shards(): return result.reshape(shot_dev, rcv_dev, samples).astype(F32)  1.48 us
    convert_element_type x1, other arithmetic, shards(): return result.reshape(shot_dev, rcv_dev, samples).astype(F32)  1.25 us

profile of v8, /device:TPU:1, one launch (start us, length us, event | category | flops | bytes accessed | tf_op | source)
XLA Modules:
  0.0 30.7 jit_solution(1736243181505206010)
XLA Ops:
  0.0 27.9 %shard_map.55 = bf16[2,12,8,16,128]{4,3,2,1,0:T(8,128)(2,1)} custom-call(bf16[4,96,1024]{2,1,0:T(8,128)(2,1)} %traces_hbm.1, s32[4,96]{1,0:T(4,128)} %dest_hbm.1, s32[4,96]{1,0:T(4,128)} %fold_hbm.1, bf16[15,4,31]{2,1,0:T(4,128)(2,1)} %bitcast.9, bf16[15,4,31]{2,1,0:T(4,128)(2,1)} %bitcast.10), custom_call_target="tpu_custom_call" | custom-call | flops 7000000000 | bytes 4000000 | tf_op jit(solution)/shard_map/pallas_call | solution.py:485
  27.9 1.2 %convert_bitcast_fusion = f32[2,2,96,8,128]{4,3,1,2,0:T(8,128)S(1)} fusion(bf16[2,96,2,8,128]{4,3,2,1,0:T(8,128)(2,1)} %bitcast.8), kind=kLoop, calls=%fused_computation | loop fusion | flops 393216 | bytes 2359296 | tf_op jit(solution)/shard_map/convert_element_type | solution.py:531
  29.2 0.1 copy.6
  29.3 1.4 %reshape.6 = f32[4,96,1024]{2,1,0:T(8,128)} reshape(f32[2,2,96,8,128]{4,3,2,1,0:T(8,128)S(1)} %copy.6) | data formatting | bytes 3145728 | tf_op jit(solution)/shard_map/convert_element_type | solution.py:531

commit v9 on v8

--- a/solution.py
+++ b/solution.py
@@ -482,11 +482,12 @@
     fans, trace_taps, sample_taps = kernels_shot.shape
     dma = pltpu.SemaphoreType.DMA
     vmem = pltpu.VMEM
+    inputs = (traces, dest, fold, kernels_shot.transpose(1, 0, 2), kernels_rcv.transpose(1, 0, 2))
     returned = pl.pallas_call(
         functools.partial(survey_kernel, shot_size, rline_size),
         out_shape=jax.ShapeDtypeStruct((groups, share, shot_size, 16, LANES), BF16),
         in_specs=[pl.BlockSpec(memory_space=pltpu.HBM)] * 5,
-        out_specs=pl.BlockSpec(memory_space=pltpu.HBM),
+        out_specs=pl.BlockSpec(memory_space=vmem),
         scratch_shapes=[
             vmem(traces.shape, BF16),
             vmem(dest.shape, jnp.int32),
@@ -523,10 +524,10 @@
             dma((pairs + 1,)),
         ],
         compiler_params=pltpu.CompilerParams(
-            vmem_limit_bytes=61 << 20, collective_id=0, has_side_effects=True
+            vmem_limit_bytes=48 << 20, collective_id=0, has_side_effects=True
         ),
         cost_estimate=pl.CostEstimate(flops=7 * 10**9, bytes_accessed=4 * 10**6, transcendentals=0),
-    )(traces, dest, fold, kernels_shot.transpose(1, 0, 2), kernels_rcv.transpose(1, 0, 2))
+    )(*[pltpu.with_memory_space_constraint(a, pltpu.HBM) for a in inputs])
     result = returned.reshape(groups, rcv_dev, 2, CHUNKS, LANES).transpose(0, 2, 1, 3, 4)
     return result.reshape(shot_dev, rcv_dev, samples).astype(F32)
 

time: 30.8 us -> 29.4 us (0.955)
  other arithmetic: 1.25 us -> 0.12 us
    convert_element_type x1, other arithmetic: 1.25 us -> 0.12 us  [shards(): return result.reshape(shot_dev, rcv_dev, samples).astype(F32)]
where the time goes in v9:
time: 29.4 us; the launch traced here: 29.2 us
  Pallas kernels  27.6 us (94%)
  local copies, waits for them, and re-layouts  1.48 us (5%)
    pallas_call x1, Pallas kernels, shards(): pl.pallas_call(functools.partial(survey_kernel, shot_size, rline_size), o...  27.6 us
    convert_element_type x2, local copies, waits for them, and re-layouts, shards(): return result.reshape(shot_dev, rcv_dev, samples).astype(F32)  1.48 us

profile of v9, /device:TPU:1, one launch (start us, length us, event | category | flops | bytes accessed | tf_op | source)
XLA Modules:
  0.0 29.2 jit_solution(11335306484989635143)
XLA Ops:
  0.0 27.6 %shard_map.55 = bf16[2,12,8,16,128]{4,3,2,1,0:T(8,128)(2,1)S(1)} custom-call(bf16[4,96,1024]{2,1,0:T(8,128)(2,1)} %traces_hbm.1, s32[4,96]{1,0:T(4,128)} %dest_hbm.1, s32[4,96]{1,0:T(4,128)} %fold_hbm.1, bf16[15,4,31]{2,1,0:T(4,128)(2,1)} %bitcast.9, bf16[15,4,31]{2,1,0:T(4,128)(2,1)} %bitcast.10), custom_call_target="tpu_custom_call" | custom-call | flops 7000000000 | bytes 4000000 | tf_op jit(solution)/shard_map/pallas_call | solution.py:486
  27.6 0.1 convert_bitcast_fusion
  27.8 0.1 copy.6
  27.9 1.4 %reshape.6 = f32[4,96,1024]{2,1,0:T(8,128)} reshape(f32[2,2,96,8,128]{4,3,2,1,0:T(8,128)S(1)} %copy.6) | data formatting | bytes 3145728 | tf_op jit(solution)/shard_map/convert_element_type | solution.py:532

commit v10 on v9

--- a/solution.py
+++ b/solution.py
@@ -154,6 +154,8 @@
     stack_ref,
     rcv_window_ref,
     back_ref,
+    returned_ref,
+    flat_ref,
     load_sem,
     halo_send,
     halo_recv,
@@ -310,14 +312,15 @@
         @pl.when(has[1 - side])
         def _(side=side):
             halo(side).start()
-    for step in range(peers):
-        fold_copy(step, me).start()
-    fold_all_ref[me] = fold_own_ref[...]
 
     for n in range(len(portions) - 1):
         if n > 0:
             inner_blocks(n)
         send_out(n)
+        if n == 0:
+            for step in range(peers):
+                fold_copy(step, me).start()
+            fold_all_ref[me] = fold_own_ref[...]
 
     loads[1].wait()
     build_table(rcv_taps_ref, taps_rows_ref, rcv_table_ref)
@@ -345,17 +348,16 @@
 
     for step in range(peers):
         fold_copy(step, source(step)).wait_recv()
-    folds = fold_all_ref[...].reshape(shot_size * 8, LANES).astype(F32)
+    folds = jnp.concatenate([fold_all_ref[t] for t in range(shot_size)], axis=0).astype(F32)
     place = lax.broadcasted_iota(jnp.int32, (16, LANES), 0)
     place = jnp.where(place < share - 2, place + 1, jnp.where(place == share - 2, 0, place))
     take = lax.broadcasted_iota(jnp.int32, (16, LANES), 1) == place * shot_size + me
     mine = lax.dot_general(
         take.astype(F32), folds, (((1,), (1,)), ((), ())), preferred_element_type=F32
     )
-    entry = lax.broadcasted_iota(jnp.int32, (shot_size * 8, rows), 0)
-    shot = lax.broadcasted_iota(jnp.int32, (shot_size * 8, rows), 1) // CHUNKS
-    spread = ((entry // 8) * shot_dev + entry % 8 == shot) & (entry % 8 < shot_dev)
-    spread = spread.astype(F32)
+    entry = lax.broadcasted_iota(jnp.int32, (shots, rows), 0)
+    shot = lax.broadcasted_iota(jnp.int32, (shots, rows), 1) // CHUNKS
+    spread = (entry == shot).astype(F32)
     labels = jnp.dot(mine, spread, preferred_element_type=F32)
     live = jnp.sum((labels >= 0.0).astype(F32), axis=1, keepdims=True) / CHUNKS
     gains = jnp.broadcast_to(jnp.sqrt(shots / live), (16, LANES))
@@ -382,7 +384,7 @@
         return [
             pltpu.make_async_remote_copy(
                 src_ref=back_ref.at[pair, peer(step), :, pl.ds(at, count)],
-                dst_ref=out_ref.at[:, pl.ds(row, count), owner],
+                dst_ref=returned_ref.at[:, pl.ds(row, count), owner],
                 send_sem=back_send.at[pair + at, step],
                 recv_sem=back_recv.at[pair + at, step],
                 device_id={"shot": peer(step)},
@@ -395,7 +397,7 @@
         return [
             pltpu.make_async_copy(
                 back_ref.at[pair, me, :, pl.ds(at, count)],
-                out_ref.at[:, pl.ds(row, count), me],
+                returned_ref.at[:, pl.ds(row, count), me],
                 own_sem.at[pair + at],
             )
             for at, row, count in parts(pair)
@@ -448,6 +450,23 @@
             prepare(pair + 1)
         finish(pair)
 
+    for pair in range(pairs):
+        for copy in back_own(pair):
+            copy.wait()
+        for step in range(peers):
+            for copy in back_copies(pair, step, source(step)):
+                copy.wait_recv()
+        for row in order[2 * pair : 2 * pair + 2]:
+            for g in range(groups):
+                flat_ref[row, g] = returned_ref[g, row].astype(F32).reshape(shot_size * 16, LANES)
+                for s in range(2):
+                    for c in range(CHUNKS):
+                        out_ref[
+                            2 * g + s,
+                            row * shot_size : (row + 1) * shot_size,
+                            c * LANES : (c + 1) * LANES,
+                        ] = flat_ref[row, g, pl.ds(s * CHUNKS + c, shot_size, stride=16)]
+
     for side in range(2):
 
         @pl.when(has[1 - side])
@@ -458,14 +477,9 @@
         fold_copy(step, me).wait_send()
         for n in range(len(portions)):
             out_copy(peer(step), n, me).wait_send()
-    for pair in range(pairs):
-        for copy in back_own(pair):
-            copy.wait()
-        for step in range(peers):
+        for pair in range(pairs):
             for copy in back_copies(pair, step, me):
                 copy.wait_send()
-            for copy in back_copies(pair, step, source(step)):
-                copy.wait_recv()
 
 
 def shards(traces, kernels_shot, kernels_rcv, dest, gather, fold, counts):
@@ -483,9 +497,9 @@
     dma = pltpu.SemaphoreType.DMA
     vmem = pltpu.VMEM
     inputs = (traces, dest, fold, kernels_shot.transpose(1, 0, 2), kernels_rcv.transpose(1, 0, 2))
-    returned = pl.pallas_call(
+    return pl.pallas_call(
         functools.partial(survey_kernel, shot_size, rline_size),
-        out_shape=jax.ShapeDtypeStruct((groups, share, shot_size, 16, LANES), BF16),
+        out_shape=jax.ShapeDtypeStruct(traces.shape, F32),
         in_specs=[pl.BlockSpec(memory_space=pltpu.HBM)] * 5,
         out_specs=pl.BlockSpec(memory_space=vmem),
         scratch_shapes=[
@@ -503,8 +517,8 @@
             vmem((2, 1024, 256), BF16),
             vmem((2, groups, RIM, 16, LANES), BF16),
             vmem((2, groups, RIM, 16, LANES), BF16),
-            vmem((8, LANES), jnp.int32),
-            vmem((shot_size, 8, LANES), jnp.int32),
+            vmem((shot_dev, LANES), jnp.int32),
+            vmem((shot_size, shot_dev, LANES), jnp.int32),
             vmem((share, CHUNKS, LANES), F32),
             vmem((share, rows, rows), BF16),
             vmem((shot_size, share, groups, 16, LANES), BF16),
@@ -512,6 +526,8 @@
             vmem((2, (shots + 16) * 16 + 16, LANES), F32),
             vmem((2, 4, shots // 2 + 8, 16, LANES), BF16),
             vmem((pairs, shot_size, groups, 2, 16, LANES), BF16),
+            vmem((groups, share, shot_size, 16, LANES), BF16),
+            vmem((share, groups, shot_size * 16, LANES), F32),
             dma((4 + shot_dev,)),
             dma((2,)),
             dma((2,)),
@@ -528,8 +544,6 @@
         ),
         cost_estimate=pl.CostEstimate(flops=7 * 10**9, bytes_accessed=4 * 10**6, transcendentals=0),
     )(*[pltpu.with_memory_space_constraint(a, pltpu.HBM) for a in inputs])
-    result = returned.reshape(groups, rcv_dev, 2, CHUNKS, LANES).transpose(0, 2, 1, 3, 4)
-    return result.reshape(shot_dev, rcv_dev, samples).astype(F32)
 
 
 def solution(mesh):

time: 29.4 us -> 29.2 us (level)
  local copies, waits for them, and re-layouts: 1.48 us -> 1.15 us
    convert_element_type x2 -> x0, local copies, waits for them, and re-layouts: 1.48 us -> none  [shards(): return result.reshape(shot_dev, rcv_dev, samples).astype(F32)]
    unnamed x0 -> x1, local copies, waits for them, and re-layouts: none -> 1.15 us
where the time goes in v10:
time: 29.2 us; the launch traced here: 29 us
  Pallas kernels  27.8 us (95%)
  local copies, waits for them, and re-layouts  1.15 us (4%)
    pallas_call x1, Pallas kernels, shards(): pl.pallas_call(functools.partial(survey_kernel, shot_size, rline_size), o...  27.8 us
    unnamed x1, local copies, waits for them, and re-layouts  1.15 us

profile of v10, /device:TPU:1, one launch (start us, length us, event | category | flops | bytes accessed | tf_op | source)
XLA Modules:
  0.0 29.0 jit_solution(14356991760492058374)
XLA Ops:
  0.0 27.8 %shard_map.55 = f32[4,96,1024]{2,1,0:T(8,128)S(1)} custom-call(bf16[4,96,1024]{2,1,0:T(8,128)(2,1)} %traces_hbm.1, s32[4,96]{1,0:T(4,128)} %dest_hbm.1, s32[4,96]{1,0:T(4,128)} %fold_hbm.1, bf16[15,4,31]{2,1,0:T(4,128)(2,1)} %bitcast.2, bf16[15,4,31]{2,1,0:T(4,128)(2,1)} %bitcast.3), custom_call_target="tpu_custom_call" | custom-call | flops 7000000000 | bytes 4000000 | tf_op jit(solution)/shard_map/pallas_call | solution.py:500
  27.9 1.1 %copy.7 = f32[4,96,1024]{2,1,0:T(8,128)} copy(f32[4,96,1024]{2,1,0:T(8,128)S(1)} %shard_map.55) | data formatting | bytes 3145728

commit v11 on v10

--- a/solution.py
+++ b/solution.py
@@ -224,16 +224,21 @@
     mask_ref[...] = lax.dot_general(
         alive_ref[...], pick_shot.astype(F32), (((0,), (0,)), ((), ())), preferred_element_type=F32
     )
+    def relayout(tiles):
+        for s in range(shot_dev):
+            for i in tiles:
+                x = traces_ref[s, pl.ds(i * 16, 16)].astype(F32)
+                for half in range(2):
+                    mask = mask_ref[i * 16 + half * 8 : i * 16 + half * 8 + 8, s * LANES : (s + 1) * LANES]
+                    begin = (i * 16 + half * 8 + RIM) * 16 + 8 + (s % 2) * CHUNKS
+                    for c in range(CHUNKS):
+                        piece = x[half * 8 : half * 8 + 8, c * LANES : (c + 1) * LANES]
+                        plain_ref[s // 2, pl.ds(begin + c, 8, stride=16)] = piece * mask
+
     for s in range(shot_dev):
         loads[4 + s].wait()
-        for i in range(receivers // 16):
-            x = traces_ref[s, pl.ds(i * 16, 16)].astype(F32)
-            for half in range(2):
-                mask = mask_ref[i * 16 + half * 8 : i * 16 + half * 8 + 8, s * LANES : (s + 1) * LANES]
-                begin = (i * 16 + half * 8 + RIM) * 16 + 8 + (s % 2) * CHUNKS
-                for c in range(CHUNKS):
-                    piece = x[half * 8 : half * 8 + 8, c * LANES : (c + 1) * LANES]
-                    plain_ref[s // 2, pl.ds(begin + c, 8, stride=16)] = piece * mask
+    last_tile = receivers // 16 - 1
+    relayout([0, 1, last_tile])
 
     for g in range(groups):
         for side, begin in enumerate((receivers - RIM, 0)):
@@ -314,6 +319,8 @@
             halo(side).start()
 
     for n in range(len(portions) - 1):
+        if n == 1:
+            relayout(range(2, last_tile))
         if n > 0:
             inner_blocks(n)
         send_out(n)

time: 29.2 us -> 29.1 us (level)
  no operation moved by 1% of the time
where the time goes in v11:
time: 29.1 us; the launch traced here: 29 us
  Pallas kernels  27.8 us (96%)
  local copies, waits for them, and re-layouts  1.15 us (4%)
    pallas_call x1, Pallas kernels, shards(): pl.pallas_call(functools.partial(survey_kernel, shot_size, rline_size), o...  27.8 us
    unnamed x1, local copies, waits for them, and re-layouts  1.15 us

profile of v11, /device:TPU:1, one launch (start us, length us, event | category | flops | bytes accessed | tf_op | source)
XLA Modules:
  0.0 29.0 jit_solution(4760647834886942496)
XLA Ops:
  0.0 27.8 %shard_map.55 = f32[4,96,1024]{2,1,0:T(8,128)S(1)} custom-call(bf16[4,96,1024]{2,1,0:T(8,128)(2,1)} %traces_hbm.1, s32[4,96]{1,0:T(4,128)} %dest_hbm.1, s32[4,96]{1,0:T(4,128)} %fold_hbm.1, bf16[15,4,31]{2,1,0:T(4,128)(2,1)} %bitcast.2, bf16[15,4,31]{2,1,0:T(4,128)(2,1)} %bitcast.3), custom_call_target="tpu_custom_call" | custom-call | flops 7000000000 | bytes 4000000 | tf_op jit(solution)/shard_map/pallas_call | solution.py:507
  27.8 1.1 %copy.7 = f32[4,96,1024]{2,1,0:T(8,128)} copy(f32[4,96,1024]{2,1,0:T(8,128)S(1)} %shard_map.55) | data formatting | bytes 3145728

commit v12 on v11

--- a/solution.py
+++ b/solution.py
@@ -383,32 +383,18 @@
         end = (RIM + shots) * 16 + 8
         stack_ref[slot, end:] = jnp.zeros((stack_ref.shape[1] - end, LANES), F32)
 
-    def parts(pair):
-        one, two = order[2 * pair], order[2 * pair + 1]
-        return [(0, one, 2)] if two == one + 1 else [(0, one, 1), (1, two, 1)]
-
-    def back_copies(pair, step, owner):
-        return [
-            pltpu.make_async_remote_copy(
-                src_ref=back_ref.at[pair, peer(step), :, pl.ds(at, count)],
-                dst_ref=returned_ref.at[:, pl.ds(row, count), owner],
-                send_sem=back_send.at[pair + at, step],
-                recv_sem=back_recv.at[pair + at, step],
-                device_id={"shot": peer(step)},
-                device_id_type=MESH,
-            )
-            for at, row, count in parts(pair)
-        ]
+    def back_copy(pair, step, owner):
+        return pltpu.make_async_remote_copy(
+            src_ref=back_ref.at[pair, peer(step)],
+            dst_ref=returned_ref.at[pair, owner],
+            send_sem=back_send.at[pair, step],
+            recv_sem=back_recv.at[pair, step],
+            device_id={"shot": peer(step)},
+            device_id_type=MESH,
+        )
 
     def back_own(pair):
-        return [
-            pltpu.make_async_copy(
-                back_ref.at[pair, me, :, pl.ds(at, count)],
-                returned_ref.at[:, pl.ds(row, count), me],
-                own_sem.at[pair + at],
-            )
-            for at, row, count in parts(pair)
-        ]
+        return pltpu.make_async_copy(back_ref.at[pair, me], returned_ref.at[pair, me], own_sem.at[pair])
 
     def prepare(pair):
         slot = pair % 2
@@ -437,10 +423,8 @@
             )
             back_ref[pair, :, :, side] = back.astype(BF16).reshape(shot_size, groups, 16, LANES)
         for step in range(peers):
-            for copy in back_copies(pair, step, me):
-                copy.start()
-        for copy in back_own(pair):
-            copy.start()
+            back_copy(pair, step, me).start()
+        back_own(pair).start()
 
     def arrive(n):
         for step in range(peers):
@@ -458,14 +442,12 @@
         finish(pair)
 
     for pair in range(pairs):
-        for copy in back_own(pair):
-            copy.wait()
+        back_own(pair).wait()
         for step in range(peers):
-            for copy in back_copies(pair, step, source(step)):
-                copy.wait_recv()
-        for row in order[2 * pair : 2 * pair + 2]:
+            back_copy(pair, step, source(step)).wait_recv()
+        for side, row in enumerate(order[2 * pair : 2 * pair + 2]):
             for g in range(groups):
-                flat_ref[row, g] = returned_ref[g, row].astype(F32).reshape(shot_size * 16, LANES)
+                flat_ref[row, g] = returned_ref[pair, :, g, side].astype(F32).reshape(shot_size * 16, LANES)
                 for s in range(2):
                     for c in range(CHUNKS):
                         out_ref[
@@ -485,8 +467,7 @@
         for n in range(len(portions)):
             out_copy(peer(step), n, me).wait_send()
         for pair in range(pairs):
-            for copy in back_copies(pair, step, me):
-                copy.wait_send()
+            back_copy(pair, step, me).wait_send()
 
 
 def shards(traces, kernels_shot, kernels_rcv, dest, gather, fold, counts):
@@ -533,7 +514,7 @@
             vmem((2, (shots + 16) * 16 + 16, LANES), F32),
             vmem((2, 4, shots // 2 + 8, 16, LANES), BF16),
             vmem((pairs, shot_size, groups, 2, 16, LANES), BF16),
-            vmem((groups, share, shot_size, 16, LANES), BF16),
+            vmem((pairs, shot_size, groups, 2, 16, LANES), BF16),
             vmem((share, groups, shot_size * 16, LANES), F32),
             dma((4 + shot_dev,)),
             dma((2,)),
@@ -542,9 +523,9 @@
             dma((peers,)),
             dma((shot_size, 4)),
             dma((shot_size, 4)),
-            dma((pairs + 1, peers)),
-            dma((pairs + 1, peers)),
-            dma((pairs + 1,)),
+            dma((pairs, peers)),
+            dma((pairs, peers)),
+            dma((pairs,)),
         ],
         compiler_params=pltpu.CompilerParams(
             vmem_limit_bytes=48 << 20, collective_id=0, has_side_effects=True

time: 29.1 us -> 29 us (level)
  no operation moved by 1% of the time
where the time goes in v12:
time: 29 us; the launch traced here: 28.8 us
  Pallas kernels  27.7 us (96%)
  local copies, waits for them, and re-layouts  1.15 us (4%)
    pallas_call x1, Pallas kernels, shards(): pl.pallas_call(functools.partial(survey_kernel, shot_size, rline_size), o...  27.7 us
    unnamed x1, local copies, waits for them, and re-layouts  1.15 us

profile of v12, /device:TPU:1, one launch (start us, length us, event | category | flops | bytes accessed | tf_op | source)
XLA Modules:
  0.0 28.8 jit_solution(12430332829284665818)
XLA Ops:
  0.0 27.7 %shard_map.55 = f32[4,96,1024]{2,1,0:T(8,128)S(1)} custom-call(bf16[4,96,1024]{2,1,0:T(8,128)(2,1)} %traces_hbm.1, s32[4,96]{1,0:T(4,128)} %dest_hbm.1, s32[4,96]{1,0:T(4,128)} %fold_hbm.1, bf16[15,4,31]{2,1,0:T(4,128)(2,1)} %bitcast.2, bf16[15,4,31]{2,1,0:T(4,128)(2,1)} %bitcast.3), custom_call_target="tpu_custom_call" | custom-call | flops 7000000000 | bytes 4000000 | tf_op jit(solution)/shard_map/pallas_call | solution.py:488
  27.7 1.1 %copy.7 = f32[4,96,1024]{2,1,0:T(8,128)} copy(f32[4,96,1024]{2,1,0:T(8,128)S(1)} %shard_map.55) | data formatting | bytes 3145728

commit v13 on v12

--- a/solution.py
+++ b/solution.py
@@ -312,11 +312,6 @@
 
     inner_blocks(0)
     pl.semaphore_wait(barrier, peers + has[0].astype(jnp.int32) + has[1].astype(jnp.int32))
-    for side in range(2):
-
-        @pl.when(has[1 - side])
-        def _(side=side):
-            halo(side).start()
 
     for n in range(len(portions) - 1):
         if n == 1:
@@ -325,6 +320,12 @@
             inner_blocks(n)
         send_out(n)
         if n == 0:
+            for side in range(2):
+
+                @pl.when(has[1 - side])
+                def _(side=side):
+                    halo(side).start()
+
             for step in range(peers):
                 fold_copy(step, me).start()
             fold_all_ref[me] = fold_own_ref[...]

time: 29 us -> 29 us (level)
  no operation moved by 1% of the time
where the time goes in v13:
time: 29 us; the launch traced here: 28.8 us
  Pallas kernels  27.7 us (96%)
  local copies, waits for them, and re-layouts  1.15 us (4%)
    pallas_call x1, Pallas kernels, shards(): pl.pallas_call(functools.partial(survey_kernel, shot_size, rline_size), o...  27.7 us
    unnamed x1, local copies, waits for them, and re-layouts  1.15 us

profile of v13, /device:TPU:1, one launch (start us, length us, event | category | flops | bytes accessed | tf_op | source)
XLA Modules:
  0.0 28.8 jit_solution(14584364030101967219)
XLA Ops:
  0.0 27.7 %shard_map.55 = f32[4,96,1024]{2,1,0:T(8,128)S(1)} custom-call(bf16[4,96,1024]{2,1,0:T(8,128)(2,1)} %traces_hbm.1, s32[4,96]{1,0:T(4,128)} %dest_hbm.1, s32[4,96]{1,0:T(4,128)} %fold_hbm.1, bf16[15,4,31]{2,1,0:T(4,128)(2,1)} %bitcast.2, bf16[15,4,31]{2,1,0:T(4,128)(2,1)} %bitcast.3), custom_call_target="tpu_custom_call" | custom-call | flops 7000000000 | bytes 4000000 | tf_op jit(solution)/shard_map/pallas_call | solution.py:489
  27.7 1.1 %copy.7 = f32[4,96,1024]{2,1,0:T(8,128)} copy(f32[4,96,1024]{2,1,0:T(8,128)S(1)} %shard_map.55) | data formatting | bytes 3145728
